TPU v7x, 512 devices: a whole 4x4x16 slice. The times are simulated.
512 devices in a mesh: ctx: 64 (over x, z), head: 8 (over y, core).
Axes of the slice: x: 4, y: 4, z: 16, core: 2. Of those that a mesh axis runs over, the one named last changes fastest.
Arguments:
- queries: bfloat16 [8192, 8192], P('ctx', 'head'), may hold values from -8 to 8
- keys: bfloat16 [8192, 1024], P('ctx', 'head'), may hold values from -8 to 8
- values: bfloat16 [8192, 1024], P('ctx', 'head'), may hold values from -12 to 12
- tile_mask: int32 [8, 64, 64], P('head'), may hold values from 0 to 1, as said below
Outputs:
- attn_out: bfloat16 [8192, 8192], P('ctx', 'head')
- key_coeffs: float32 [8192, 160], P('ctx')
- key_factor: float32 [160, 1024], P(None, 'head')
Inputs may be any that keep to these rules, and one draw needn't show every extreme that they name: tile_mask[h, i, j] is 1 exactly where j <= i and either j is one of 4 vertical tiles of head h (tile 0 among them) or i - j is one of 4 diagonal offsets of head h (offset 0 among them).
All inputs are finite; a program needn't handle non-finite values.
Results may differ from a plain program's by a relative error of at most 0.011.
Values may be sent and summed in bfloat16 or wider, within the bound.
No kernel may reach another device: no remote copies, remote signals or barrier semaphores. Data moves between devices by JAX's collectives and lax.ppermute only.
A program may use at most 64 MiB of HBM per device.

v0:
```python
import math

import jax
import jax.numpy as jnp
from jax import lax
from jax.sharding import PartitionSpec as P

HD = 128
GQ = 8
TILE = 128
PIVOTS = 20


NEG = -1e30
ROPE_BASE = 500000.0


def angles(positions, width):
    inverse = jnp.exp(
        -math.log(ROPE_BASE) * 2.0 * jnp.arange(width // 2, dtype=jnp.float32) / width
    )
    turning = positions[:, None] * inverse[None, :]
    turning = jnp.concatenate([turning, turning], axis=1)
    return (jnp.cos(turning), jnp.sin(turning))


def rotate(head_vals, cosine, sine):
    shape = (cosine.shape[0],) + (1,) * (head_vals.ndim - 2) + (cosine.shape[1],)
    half_size = head_vals.shape[-1] // 2
    turned = jnp.concatenate([-head_vals[..., half_size:], head_vals[..., :half_size]], axis=-1)
    return head_vals * cosine.reshape(shape) + turned * sine.reshape(shape)


def on_device(queries, keys, values, tile_mask):
    ctx_size = lax.axis_size("ctx")
    ctx_index = lax.axis_index("ctx")
    tok_rows = keys.shape[0]
    local_heads = tile_mask.shape[0]
    tile_total = tile_mask.shape[1]
    token_total = tok_rows * ctx_size
    positions = ctx_index * tok_rows + lax.iota(jnp.int32, tok_rows)
    cosine, sine = angles(positions.astype(jnp.float32), HD)
    rot_queries = rotate(
        queries.reshape(tok_rows, local_heads, GQ, HD).astype(jnp.float32), cosine, sine
    ).astype(jnp.bfloat16)
    rot_keys = rotate(
        keys.reshape(tok_rows, local_heads, HD).astype(jnp.float32), cosine, sine
    ).astype(jnp.bfloat16)
    value_heads = values.reshape(tok_rows, local_heads, HD)
    pivot_local = keys.reshape(tok_rows, local_heads, HD)[:, :, :PIVOTS].reshape(
        tok_rows, local_heads * PIVOTS
    )
    pivots = lax.all_gather(pivot_local, "head", axis=1, tiled=True)
    cross_part = jnp.dot(pivots.T, keys, preferred_element_type=jnp.float32)
    gram_part = jnp.dot(pivots.T, pivots, preferred_element_type=jnp.float32)
    gram_sum, cross_sum = lax.psum((gram_part, cross_part), "ctx")
    lower_factor = jnp.linalg.cholesky(gram_sum / token_total)
    key_factor = jax.scipy.linalg.solve_triangular(
        lower_factor, cross_sum / token_total, lower=True
    )
    key_coeffs = jax.scipy.linalg.solve_triangular(
        lower_factor, pivots.astype(jnp.float32).T, lower=True
    ).T
    score_scale = HD ** (-0.5)
    tile_ids = lax.iota(jnp.int32, tile_total)
    mask_float = tile_mask.astype(jnp.float32)
    row_pick = (positions[:, None] // TILE == tile_ids[None, :]).astype(jnp.float32)
    tile_rows = jnp.einsum("rt,htu->hru", row_pick, mask_float)
    groups = [(rot_queries, positions, tile_rows)]

    def absorb(softmax_state, query_group, keys_blk, values_blk, key_pos):
        query_rows, query_pos, tile_rows = query_group
        col_pick = (key_pos[:, None] // TILE == tile_ids[None, :]).astype(jnp.float32)
        allowed = (jnp.einsum("hru,ku->hrk", tile_rows, col_pick) > 0.5) & (
            key_pos[None, None, :] <= query_pos[None, :, None]
        )
        running_max, totals, accum = softmax_state
        scores = (
            jnp.einsum("rhgd,khd->hgrk", query_rows, keys_blk, preferred_element_type=jnp.float32)
            * score_scale
        )
        permit = allowed[:, None]
        scores = jnp.where(permit, scores, NEG)
        new_max = jnp.maximum(running_max, jnp.max(scores, axis=-1))
        weights = jnp.where(permit, jnp.exp(scores - new_max[..., None]), 0.0)
        rescale = jnp.exp(running_max - new_max)
        totals = totals * rescale + jnp.sum(weights, axis=-1)
        summed = jnp.einsum(
            "hgrk,khd->rhgd",
            weights.astype(jnp.bfloat16),
            values_blk,
            preferred_element_type=jnp.float32,
        )
        accum = accum * jnp.transpose(rescale, (2, 0, 1))[..., None] + summed
        return (new_max, totals, accum)

    initial = tuple(
        (
            (
                jnp.full((local_heads, GQ, one_group[0].shape[0]), NEG, jnp.float32),
                jnp.zeros((local_heads, GQ, one_group[0].shape[0]), jnp.float32),
                jnp.zeros((one_group[0].shape[0], local_heads, GQ, HD), jnp.float32),
            )
            for one_group in groups
        )
    )
    keys_part = lax.all_gather(rot_keys, "ctx", axis=0, tiled=True)
    values_part = lax.all_gather(value_heads, "ctx", axis=0, tiled=True)
    piece_rows = keys_part.shape[0]
    block_rows = math.gcd(piece_rows, 1024)

    def block_step(step_index, inner_state):
        offset = step_index * block_rows
        keys_blk = lax.dynamic_slice_in_dim(keys_part, offset, block_rows, 0)
        values_blk = lax.dynamic_slice_in_dim(values_part, offset, block_rows, 0)
        key_pos = offset + lax.iota(jnp.int32, block_rows)
        return tuple(
            (
                absorb(one_state, one_group, keys_blk, values_blk, key_pos)
                for one_state, one_group in zip(inner_state, groups)
            )
        )

    finished = lax.fori_loop(0, piece_rows // block_rows, block_step, initial)
    results = []
    for one_state in finished:
        running_max, totals, accum = one_state
        normed = (accum / jnp.transpose(totals, (2, 0, 1))[..., None]).astype(jnp.bfloat16)
        results.append(normed.reshape(normed.shape[0], local_heads * GQ * HD))
    attn_out = results[0]
    return (attn_out, key_coeffs, key_factor)


def solution(mesh):
    return jax.shard_map(
        on_device,
        mesh=mesh,
        in_specs=(P("ctx", "head"), P("ctx", "head"), P("ctx", "head"), P("head", None, None)),
        out_specs=(P("ctx", "head"), P("ctx", None), P(None, "head")),
        check_vma=False,
    )
```

profile of v0, /device:TPU:1, one launch (start us, length us, event | category | flops | bytes accessed | tf_op | source)
XLA Modules:
  0.0 640.6 jit_solution(4084793734556822813)
XLA Ops:
  7.2 0.8 copy.42
  8.1 19.5 %all-gather.2 = bf16[128,1,160]{0,1,2:T(2,128)(2,1)S(1)} all-gather(bf16[128,1,20]{0,1,2:T(2,128)(2,1)S(1)} %copy.42), channel_id=4, replica_groups=mesh['ctx'=64,'head'=8] {'head'}, dimensions={2}, use_global_device_ids=true | all-gather | bytes 46080 | tf_op jit(solution)/shard_map/all_gather | solution.py:53
  27.5 0.9 fusion.53
  28.4 1.5 fusion.51
  30.0 0.8 convert_bitcast_fusion
  31.0 1.7 fusion.50
  32.7 1.5 copy.38
  34.2 1.1 copy.35
  36.2 243.3 %all-reduce.6.cloned.1.call-done = (f32[160,160]{0,1:T(8,128)}, f32[160,128]{1,0:T(8,128)}) async-done(((f32[160,160]{0,1:T(8,128)}, f32[160,128]{1,0:T(8,128)}), (f32[160,160]{0,1:T(8,128)}, f32[160,128]{1,0:T(8,128)})) %all-reduce.6.cloned.1.call-update) | async-done | bytes 184336 | tf_op jit(solution)/shard_map/psum | solution.py:56
  279.5 0.9 broadcast_multiply_fusion
  280.6 1.0 fusion.38
  281.6 11.7 %cholesky.51 = f32[128,128]{1,0:T(8,128)S(1)} custom-call(f32[128,128]{1,0:T(8,128)S(1)} %cholesky.124), custom_call_target="Cholesky" | custom-call | tf_op jit(solution)/shard_map/jit(cholesky)/cholesky | solution.py:57
  293.3 9.8 %custom-call.14 = f32[1,128,128]{1,2,0:T(8,128)S(1)} custom-call(f32[1,128,128]{2,1,0:T(8,128)S(1)} %get-tuple-element.374), custom_call_target="InvertDiagBlocksLowerTriangular" | custom-call | tf_op jit(solution)/shard_map/jit(cholesky)/cholesky | solution.py:57
  303.5 2.9 cholesky.110
  306.4 0.6 compare_reduce_fusion.1
  307.1 0.6 compare_reduce_fusion
  309.1 19.9 %custom-call.19 = f32[2,128,128]{1,2,0:T(8,128)S(1)} custom-call(f32[2,128,128]{2,1,0:T(8,128)S(1)} %pad_maximum_fusion), custom_call_target="InvertDiagBlocksLowerTriangular" | custom-call | tf_op jit(solution)/shard_map/jit(_solve_triangular)/triangular_solve | solution.py:61
  329.7 0.6 maximum_bitcast_fusion
  330.3 0.9 broadcast_multiply_fusion.1
  331.9 0.6 pad_maximum_fusion.1
  332.6 88.5 %all-gather.6.cloned.1.call-done = bf16[8192,128]{1,0:T(8,128)(2,1)} async-done(((bf16[128,128]{1,0:T(8,128)(2,1)}), bf16[8192,128]{1,0:T(8,128)(2,1)}) %all-gather.6.cloned.1.call-update) | async-done | bytes 2097168 | tf_op jit(solution)/shard_map/all_gather | solution.py:107
  421.0 134.4 %all-gather.8.cloned.1.call-done = bf16[8192,128]{0,1:T(8,128)(2,1)} async-done(((bf16[128,128]{0,1:T(8,128)(2,1)}), bf16[8192,128]{0,1:T(8,128)(2,1)}) %all-gather.8.cloned.1.call-update) | async-done | bytes 2097168 | tf_op jit(solution)/shard_map/all_gather | solution.py:108
  555.4 77.8 %while.23 = (s32[]{:T(128)}, f32[1,8,128]{2,1,0:T(8,128)S(1)}, f32[1,8,128]{2,1,0:T(8,128)S(1)}, f32[128,1,8,128]{0,3,2,1:T(8,128)S(1)}, bf16[1,128,64]{2,1,0:T(...) while((s32[]{:T(128)}, f32[1,8,128]{2,1,0:T(8,128)S(1)}, ...), condition=%wide.region_3.4_spmd.clone, body=%wide.region_0.3_spmd.clone.sunk | while | flops 568154240 | bytes 31818984 | solution.py:124
  555.8 3.6 fusion.85
  559.5 3.3 fusion.87
  562.9 2.2 fusion.88
  565.5 3.6 fusion.85
  569.2 3.3 fusion.87
  572.6 2.2 fusion.88
  575.2 3.6 fusion.85
  578.9 3.3 fusion.87
  582.3 2.2 fusion.88
  585.0 3.7 fusion.85
  588.6 3.3 fusion.87
  592.1 2.2 fusion.88
  594.7 3.7 fusion.85
  598.4 3.3 fusion.87
  601.8 2.2 fusion.88
  604.4 3.7 fusion.85
  608.1 3.3 fusion.87
  611.5 2.2 fusion.88
  614.1 3.7 fusion.85
  617.8 3.3 fusion.87
  621.2 2.2 fusion.88
  623.9 3.7 fusion.85
  627.5 3.3 fusion.87
  631.0 2.2 fusion.88
  633.3 0.9 copy.47
  (109 shorter events, 6.7 us)
Async XLA Ops:
  7.2 28.5 %copy-start.1 = (s32[1,64,64]{2,1,0:T(8,128)S(1)}, s32[1,64,64]{2,1,0:T(8,128)}, u32[]{:S(2)}) copy-start(s32[1,64,64]{2,1,0:T(8,128)} %param.11) | copy-start | bytes 49156
  7.2 272.4 %all-reduce.6.cloned.1.call-start = ((), (), s32[]{:S(2)}) async-start(), calls=%async_computation.2 | async-start | bytes 491520 | tf_op jit(solution)/shard_map/psum | solution.py:56
  29.9 391.1 %all-gather.6.cloned.1.call-start = ((), (), s32[]{:S(2)}) async-start(), calls=%async_computation | async-start | bytes 2129920 | tf_op jit(solution)/shard_map/all_gather | solution.py:107
  32.7 522.7 %all-gather.8.cloned.1.call-start = ((), (), s32[]{:S(2)}) async-start(), calls=%async_computation.1 | async-start | bytes 2129920 | tf_op jit(solution)/shard_map/all_gather | solution.py:108
  559.4 3.4 copy-start
  569.2 3.4 copy-start
  578.9 3.4 copy-start
  588.6 3.4 copy-start
  598.3 3.4 copy-start
  608.1 3.4 copy-start
  617.8 3.4 copy-start
  627.5 3.4 copy-start
Sparse Core Ops, SparseCore 0:
  30.1 249.4 all-reduce.5
  282.9 138.0 all-gather.5
  424.4 131.0 all-gather.7
where the time goes:
time: 650 us; the launch traced here: 641 us
  waiting for transfers between devices  466 us (72%)
  other arithmetic  79.7 us (12%)
  matrix products  53.9 us (8%)
  blocking collectives  19.5 us (3%)
  between operations  15.4 us (2%)
    psum x1, waiting for transfers between devices, on_device(): gram_sum, cross_sum = lax.psum((gram_part, cross_part), 'ctx')  243 us
    all_gather x1, waiting for transfers between devices, on_device(): values_part = lax.all_gather(value_heads, 'ctx', axis=0, tiled=True)  134 us
    all_gather x1, waiting for transfers between devices, on_device(): keys_part = lax.all_gather(rot_keys, 'ctx', axis=0, tiled=True)  88.5 us
    dot_general x8, matrix products, absorb(): jnp.einsum('rhgd,khd->hgrk', query_rows, keys_blk, preferred_element_type...  29.2 us
    reduce_sum x8, other arithmetic, absorb(): totals = totals * rescale + jnp.sum(weights, axis=-1)  26.7 us
    another operation x7, other arithmetic, on_device(): lower_factor = jnp.linalg.cholesky(gram_sum / token_total)  25.8 us
    another operation x6, other arithmetic, on_device(): jax.scipy.linalg.solve_triangular(lower_factor, pivots.astype(jnp.float32...  20 us
    all_gather x1, blocking collectives, on_device(): pivots = lax.all_gather(pivot_local, 'head', axis=1, tiled=True)  19.5 us
  transfers between devices with their start and end apart: 3, of which 3 were waited for; matrix products, arithmetic and copies ran while one was open for 9% of the time, Pallas kernels for 0%

commit v1 on v0

v1 whole, which is shorter than its diff:
```python
import functools
import math

import jax
import jax.numpy as jnp
from jax import lax
from jax.experimental import pallas as pl
from jax.experimental.pallas import tpu as pltpu
from jax.sharding import PartitionSpec as P

HD = 128
GQ = 8
TILE = 128
PIVOTS = 20
NEAR = 4
FAR = 4
PANEL = 40
STRIP = 8
PIECE = 16
UNIT = 16
SLOTS = 7
NEG = -1e30
ROPE_BASE = 500000.0
VMEM_LIMIT = 48 * 1024 * 1024


def angles(positions, width):
    inverse = jnp.exp(
        -math.log(ROPE_BASE) * 2.0 * jnp.arange(width // 2, dtype=jnp.float32) / width
    )
    turning = positions[:, None] * inverse[None, :]
    cosine, sine = jnp.cos(turning), jnp.sin(turning)
    return (
        jnp.concatenate([cosine, cosine], axis=1),
        jnp.concatenate([-sine, sine], axis=1),
    )


def turn(head_vals, cosine, signed_sine):
    return head_vals * cosine + pltpu.roll(head_vals, HD // 2, 1) * signed_sine


def params():
    return pltpu.CompilerParams(vmem_limit_bytes=VMEM_LIMIT)


def iota(shape, dim):
    return lax.broadcasted_iota(jnp.int32, shape, dim)


def pivots_kernel(keys_ref, piv_ref):
    first = (iota((32, HD), 0) == iota((32, HD), 1)).astype(jnp.bfloat16)
    pivots = lax.dot_general(
        first, keys_ref[...], (((1,), (1,)), ((), ())), preferred_element_type=jnp.float32
    ).astype(jnp.bfloat16)
    for head in range(piv_ref.shape[0]):
        piv_ref[head] = pivots


def prepare_kernel(keys_ref, values_ref, cos_ref, sin_ref, kv_ref):
    keys = keys_ref[...].astype(jnp.float32)
    kv_ref[0:TILE, :] = turn(keys, cos_ref[...], sin_ref[...]).astype(jnp.bfloat16)
    kv_ref[TILE:, :] = values_ref[...]


def queries_kernel(me_ref, mask_ref, queries_ref, cos_ref, sin_ref, out_ref, bias_ref):
    cosine, sine = cos_ref[...], sin_ref[...]
    for g in range(GQ):
        lanes = slice(g * HD, (g + 1) * HD)
        query = turn(queries_ref[:, lanes].astype(jnp.float32), cosine, sine)
        out_ref[:, lanes] = query.astype(jnp.bfloat16)
    mask = mask_ref[0]
    count = jnp.sum(jnp.where(iota(mask.shape, 0) == me_ref[0], mask, 0)) - 1
    width = SLOTS * TILE
    slot = iota((TILE, width), 1) % (SLOTS * PIECE) // PIECE
    bias_ref[:, 0:width] = jnp.where(slot < count, 0.0, NEG)
    below = iota((TILE, TILE), 1) <= iota((TILE, TILE), 0)
    bias_ref[:, width:] = jnp.where(below, 0.0, NEG)


def index_kernel(stride, far_ref, mask_ref, out_ref):
    tiles = mask_ref.shape[1]
    dests = out_ref.shape[0]
    mask = mask_ref[0].astype(jnp.bfloat16)
    dest = iota((dests, tiles), 0)
    tile = dest // NEAR * FAR * NEAR + far_ref[0] * NEAR + dest % NEAR
    own = (tile == iota((dests, tiles), 1)).astype(jnp.bfloat16)
    mine = jnp.dot(own, mask, preferred_element_type=jnp.float32)
    mine = mine * (1.0 - own.astype(jnp.float32))
    before = (iota((tiles, tiles), 0) < iota((tiles, tiles), 1)).astype(jnp.bfloat16)
    rank = jnp.dot(mine.astype(jnp.bfloat16), before, preferred_element_type=jnp.float32)
    col = iota((dests, tiles), 1)
    place = col // NEAR % FAR * stride + (col // (FAR * NEAR) * NEAR + col % NEAR) * PIECE
    place = place.astype(jnp.float32) * mine
    lane = iota(out_ref.shape, 1)
    found = jnp.zeros(out_ref.shape, jnp.float32)
    for slot in range(SLOTS):
        value = jnp.sum(jnp.where(rank == slot, place, 0.0), axis=1, keepdims=True)
        found = jnp.where(lane == slot, value, found)
    out_ref[...] = found.astype(jnp.int32)


def two_terms(total):
    high = total.astype(jnp.bfloat16).astype(jnp.float32)
    return jnp.concatenate([high, total - high], axis=0).astype(jnp.bfloat16)


def one_term(terms):
    terms = terms.astype(jnp.float32)
    half = terms.shape[0] // 2
    return terms[0:half] + terms[half:]


def fold(cross, gram, all_ref):
    rank, half = gram.shape[0], 64
    rest = rank - 128
    row, lane = iota((half, 128), 0), iota((half, 128), 1)
    low = gram[half:128, 0:128]
    diagonal = jnp.sum(jnp.where(lane == row + half, low, 0.0), axis=1, keepdims=True)
    corner = jnp.concatenate(
        [gram[128:, 128:], jnp.zeros((rest, 128 - rest), jnp.float32)], axis=1
    )
    hidden = jnp.concatenate(
        [
            corner,
            pltpu.roll(corner, 128 - rest // 2, 1),
            jnp.broadcast_to(diagonal, (half, 128)),
            jnp.zeros((rank - 2 * rest - half, 128), jnp.float32),
        ],
        axis=0,
    )
    all_ref[0:rank, :] = jnp.where(iota((rank, 128), 1) < PIVOTS, hidden, cross)
    keep = (lane < half) & (lane <= row)
    all_ref[rank:rank + half, :] = jnp.where(keep, gram[0:half, 0:128], pltpu.roll(low, half, 1))
    all_ref[rank + half:, :] = gram[128:, 0:128]


def unfold(head, inverse, sums_ref, work_ref):
    rank, half = work_ref.shape[0], 64
    rest = rank - 128
    row, lane = iota((half, 128), 0), iota((half, 128), 1)
    mixed = sums_ref[rank:rank + half, :] * inverse
    turned = pltpu.roll(mixed, half, 1)
    diagonal = jnp.broadcast_to(sums_ref[2 * rest:2 * rest + half, 0:1], (half, 128)) * inverse
    top = jnp.where((lane < half) & (lane <= row), mixed, 0.0)
    low = jnp.where(
        (lane < half) | (lane > row + half), turned, jnp.where(lane == row + half, diagonal, 0.0)
    )
    one_side = jnp.concatenate([top, low], axis=0)
    other = jnp.where(iota((128, 128), 0) == iota((128, 128), 1), 0.0, one_side.T)
    work_ref[0:128, 0:128] = one_side + other
    last = sums_ref[rank + half:, :] * inverse
    work_ref[128:, 0:128] = last
    work_ref[0:128, 128:256] = jnp.concatenate(
        [last, jnp.zeros((128 - rest, 128), jnp.float32)], axis=0
    ).T
    lane = iota((rest, 128), 1)
    second = pltpu.roll(sums_ref[rest:2 * rest, :], rest // 2, 1)
    corner = jnp.where(lane < rest // 2, sums_ref[0:rest, :], second)
    work_ref[128:, 128:256] = jnp.where(lane < rest, corner * inverse, 0.0)
    own = pltpu.roll(work_ref[:, 0:256], 256 - head * PIVOTS, 1)[:, 0:128]
    work_ref[:, 256:384] = jnp.where(
        iota((rank, 128), 1) < PIVOTS, own, sums_ref[0:rank, :] * inverse
    )


def sums_kernel(piv_ref, keys_ref, kv_ref, out_ref, pivt_ref, all_ref):
    heads = piv_ref.shape[0]
    rank = heads * PIVOTS
    padded = piv_ref[...].reshape(heads * 32, TILE)
    line = iota((rank, heads * 32), 0)
    place = line // PIVOTS * 32 + line % PIVOTS
    compact = (place == iota((rank, heads * 32), 1)).astype(jnp.bfloat16)
    pivt = jnp.dot(compact, padded, preferred_element_type=jnp.float32).astype(jnp.bfloat16)
    pivt_ref[...] = pivt
    cross = jnp.dot(pivt, keys_ref[...], preferred_element_type=jnp.float32)
    gram = lax.dot_general(
        pivt, pivt, (((1,), (1,)), ((), ())), preferred_element_type=jnp.float32
    )
    fold(cross, gram, all_ref)
    for dest in range(out_ref.shape[0]):
        out_ref[dest, 0:PIECE] = kv_ref[dest * PIECE:(dest + 1) * PIECE, :]
        out_ref[dest, PIECE:] = two_terms(all_ref[dest * UNIT:(dest + 1) * UNIT, :])


def middle_kernel(in_ref, out_ref):
    near = in_ref.shape[0]
    total = one_term(in_ref[0, PIECE:])
    for source in range(1, near):
        total = total + one_term(in_ref[source, PIECE:])
    terms = two_terms(total)
    for dest in range(out_ref.shape[0]):
        for source in range(near):
            out_ref[dest, source * PIECE:(source + 1) * PIECE] = in_ref[source, 0:PIECE]
        out_ref[dest, near * PIECE:] = terms


def pick_kernel(place_ref, in_ref, out_ref):
    near, stride = out_ref.shape[0], in_ref.shape[0] // FAR
    total = one_term(in_ref[near * PIECE:stride, :])
    for far in range(1, FAR):
        total = total + one_term(in_ref[far * stride + near * PIECE:(far + 1) * stride, :])
    terms = two_terms(total)
    for dest in range(near):
        for slot in range(SLOTS):
            start = pl.multiple_of(place_ref[dest, slot], PIECE)
            out_ref[dest, slot * PIECE:(slot + 1) * PIECE] = in_ref[pl.ds(start, PIECE), :]
        out_ref[dest, SLOTS * PIECE:] = terms


def basis_steps(tokens, head, in_ref, pivt_ref, factor_ref, coeffs_ref, work_ref, sums_ref):
    rank = pivt_ref.shape[0]
    for source in range(in_ref.shape[0]):
        sums_ref[source * UNIT:(source + 1) * UNIT, :] = one_term(in_ref[source, SLOTS * PIECE:])
    unfold(head, 1.0 / tokens, sums_ref, work_ref)
    work_ref[:, 384:512] = pivt_ref[...].astype(jnp.float32)
    for first in range(0, rank, PANEL):
        block = work_ref[first:first + PANEL, :]
        for start in range(first, first + PANEL, STRIP):
            height = block.shape[0]
            columns = [
                jnp.broadcast_to(block[:, at:at + 1], (height, 128))
                for at in range(start, start + STRIP)
            ]
            for step in range(STRIP):
                root = lax.rsqrt(columns[step][step:step + 1, :])
                column = columns[step] * root
                for later in range(step + 1, STRIP):
                    columns[later] = columns[later] - column * column[later:later + 1, :]
                line = block[step:step + 1, :] * jnp.concatenate([root] * 4, axis=1)
                work_ref[start + step:start + step + 1, :] = line
                block = block - jnp.concatenate([column] * 4, axis=1) * line
                yield
            block = block[STRIP:, :]
        last = first + PANEL
        if last < rank:
            done = work_ref[first:last, :]
            update = lax.dot_general(
                done[:, 0:256], done, (((0,), (0,)), ((), ())),
                precision=lax.Precision.HIGHEST, preferred_element_type=jnp.float32,
            )
            work_ref[last:rank, :] = work_ref[last:rank, :] - update[last:rank, :]
    factor_ref[...] = work_ref[:, 256:384]
    coeffs_ref[...] = work_ref[:, 384:512]


def attend_steps(queries_ref, bias_ref, in_ref, kv_ref, out_ref):
    per_dest = SLOTS * PIECE
    half = in_ref.shape[0] // 2
    width = half * per_dest
    keys = jnp.concatenate(
        [in_ref[0:half, 0:per_dest].reshape(width, HD), kv_ref[0:TILE, :]], axis=0
    )
    values = jnp.concatenate(
        [in_ref[half:, 0:per_dest].reshape(width, HD), kv_ref[TILE:, :]], axis=0
    )
    scale = HD ** (-0.5) * math.log2(math.e)
    for g in range(GQ):
        lanes = slice(g * HD, (g + 1) * HD)
        scores = lax.dot_general(
            queries_ref[:, lanes], keys, (((1,), (1,)), ((), ())),
            preferred_element_type=jnp.float32,
        ) * scale + bias_ref[...]
        yield
        most = jnp.max(scores, axis=1, keepdims=True)
        yield
        weights = jnp.exp2(scores - most)
        totals = jnp.sum(weights, axis=1, keepdims=True)
        yield
        mixed = jnp.dot(
            weights.astype(jnp.bfloat16), values, preferred_element_type=jnp.float32
        )
        yield
        out_ref[:, lanes] = (mixed / totals).astype(jnp.bfloat16)


def finish_kernel(
    tokens, head_ref, queries_ref, bias_ref, in_ref, kv_ref, pivt_ref,
    out_ref, factor_ref, coeffs_ref, work_ref, sums_ref,
):
    basis = basis_steps(
        tokens, head_ref[0], in_ref, pivt_ref, factor_ref, coeffs_ref, work_ref, sums_ref
    )
    attend = attend_steps(queries_ref, bias_ref, in_ref, kv_ref, out_ref)
    steps = pivt_ref.shape[0]
    for step in range(steps):
        next(basis, None)
        if step % (steps // (4 * GQ)) == 0:
            next(attend, None)
    for rest in (attend, basis):
        for _ in rest:
            pass


def on_device(queries, keys, values, tile_mask):
    near_axes = ("x", "near")
    near_size = lax.axis_size(near_axes)
    far_size = lax.axis_size("far")
    head_size = lax.axis_size("head")
    far_index = lax.axis_index("far")
    ctx_index = lax.axis_index(("x", "far", "near"))
    tok_rows = keys.shape[0]
    token_total = tok_rows * near_size * far_size
    rank = head_size * PIVOTS
    positions = ctx_index * tok_rows + lax.iota(jnp.int32, tok_rows)
    cosine, sine = angles(positions.astype(jnp.float32), HD)
    shape = jax.ShapeDtypeStruct
    bf16, f32 = jnp.bfloat16, jnp.float32
    smem, vmem = pl.BlockSpec(memory_space=pltpu.SMEM), pl.BlockSpec(memory_space=pltpu.VMEM)

    def call(kernel, name, out_shape, scalars, *arrays, scratch=()):
        return pl.pallas_call(
            kernel,
            out_shape=out_shape,
            in_specs=[smem] * scalars + [vmem] * (len(arrays) - scalars),
            scratch_shapes=scratch,
            compiler_params=params(),
            name=name,
        )(*arrays)

    pivots = call(pivots_kernel, "pivots", shape((head_size, 32, TILE), bf16), 0, keys)
    pivots = lax.all_to_all(pivots, "head", 0, 0)
    kv = call(
        prepare_kernel, "prepare", shape((2 * TILE, HD), bf16), 0, keys, values, cosine, sine
    )
    stride = near_size * PIECE + 2 * UNIT
    places = call(
        functools.partial(index_kernel, stride), "index",
        shape((near_size, 128), jnp.int32), 1, far_index.reshape(1), tile_mask,
    )
    turned, bias = call(
        queries_kernel, "queries",
        (shape(queries.shape, bf16), shape((TILE, (SLOTS + 1) * TILE), f32)), 1,
        ctx_index.reshape(1), tile_mask, queries, cosine, sine,
    )
    pivots, kv, places, turned, bias, head_index = lax.optimization_barrier(
        (pivots, kv, places, turned, bias, lax.axis_index("head").reshape(1))
    )
    first, pivt = call(
        sums_kernel, "sums",
        (shape((near_size, PIECE + 2 * UNIT, HD), bf16), shape((rank, TILE), bf16)), 0,
        pivots, keys, kv,
        scratch=[pltpu.VMEM((near_size * UNIT, HD), f32)],
    )
    first = lax.all_to_all(first, near_axes, 0, 0)
    second = call(middle_kernel, "middle", shape((far_size, stride, HD), bf16), 0, first)
    second = lax.all_to_all(second, "far", 0, 0)
    third = call(
        pick_kernel, "pick", shape((near_size, SLOTS * PIECE + 2 * UNIT, HD), bf16), 1,
        places, second.reshape(far_size * stride, HD),
    )
    third = lax.all_to_all(third, near_axes, 0, 0)

    attn_out, key_factor, coeffs = call(
        functools.partial(finish_kernel, float(token_total)), "finish",
        (shape(queries.shape, bf16), shape((rank, HD), f32), shape((rank, TILE), f32)), 1,
        head_index, turned, bias, third, kv, pivt,
        scratch=[pltpu.VMEM((rank, 512), f32), pltpu.VMEM((near_size * UNIT, HD), f32)],
    )
    return (attn_out, coeffs.T, key_factor)


def solution(mesh):
    ctx_size, head_size = mesh.shape["ctx"], mesh.shape["head"]
    split = jax.sharding.Mesh(
        mesh.devices.reshape(ctx_size // (FAR * NEAR), FAR, NEAR, head_size),
        ("x", "far", "near", "head"),
    )
    ctx = ("x", "far", "near")
    return jax.shard_map(
        on_device,
        mesh=split,
        in_specs=(P(ctx, "head"), P(ctx, "head"), P(ctx, "head"), P("head", None, None)),
        out_specs=(P(ctx, "head"), P(ctx, None), P(None, "head")),
        check_vma=False,
    )
```

time: 650 us -> 90.8 us (0.14); the launches traced: 641 us -> 90.5 us
  waiting for transfers between devices: 466 us -> 3.06 us
  other arithmetic: 79.7 us -> 0.42 us
  matrix products: 53.9 us -> 0 us
  blocking collectives: 19.5 us -> 65 us
  between operations: 15.4 us -> 0.76 us
  starting transfers between devices: 0.12 us -> 10.1 us
  Pallas kernels: 0 us -> 9.67 us
    psum x1 -> x0, waiting for transfers between devices: 243 us -> none  [on_device(): gram_sum, cross_sum = lax.psum((gram_part, cross_part), 'ctx')]
    all_gather x2 -> x0, waiting for transfers between devices: 223 us -> none  [the longest x1 134 us: on_device(): values_part = lax.all_gather(value_heads, 'ctx', axis=0, tiled=True)]
    all_to_all x0 -> x3, blocking collectives: none -> 65 us  [the longest x1 27.6 us: on_device(): second = lax.all_to_all(second, 'far', 0, 0)]
    dot_general x27 -> x0, matrix products: 52.2 us -> none  [the longest x8 29.2 us: absorb(): jnp.einsum('rhgd,khd->hgrk', query_rows, keys_blk, preferred_element_type...]
    another operation x14 -> x0, other arithmetic: 46.4 us -> none  [the longest x7 25.8 us: on_device(): lower_factor = jnp.linalg.cholesky(gram_sum / token_total)]
    reduce_sum x8 -> x0, other arithmetic: 26.7 us -> none  [absorb(): totals = totals * rescale + jnp.sum(weights, axis=-1)]
    all_gather x1 -> x0, blocking collectives: 19.5 us -> none  [on_device(): pivots = lax.all_gather(pivot_local, 'head', axis=1, tiled=True)]
    all_to_all x0 -> x1, starting transfers between devices: none -> 10.1 us  [on_device(): pivots = lax.all_to_all(pivots, 'head', 0, 0)]
  transfers between devices with their start and end apart: 3 -> 1, of which waited for: 3 -> 1; matrix products, arithmetic and copies ran while one was open for 9% -> 0% of each run, Pallas kernels for 0% -> 1%
where the time goes in v1:
time: 90.8 us; the launch traced here: 90.5 us
  blocking collectives  65 us (72%)
  starting transfers between devices  10.1 us (11%)
  Pallas kernels  9.67 us (11%)
  waiting for transfers between devices  3.06 us (3%)
  local copies, waits for them, and re-layouts  1.38 us (2%)
    all_to_all x1, blocking collectives, on_device(): second = lax.all_to_all(second, 'far', 0, 0)  27.6 us
    all_to_all x1, blocking collectives, on_device(): third = lax.all_to_all(third, near_axes, 0, 0)  26.1 us
    all_to_all x1, blocking collectives, on_device(): first = lax.all_to_all(first, near_axes, 0, 0)  11.3 us
    all_to_all x1, starting transfers between devices, on_device(): pivots = lax.all_to_all(pivots, 'head', 0, 0)  10.1 us
    pallas_call x8, Pallas kernels, call(): pl.pallas_call(kernel, out_shape=out_shape, in_specs=[smem] * scalars + [...  9.67 us
    all_to_all x1, waiting for transfers between devices, on_device(): pivots = lax.all_to_all(pivots, 'head', 0, 0)  3.06 us
  transfers between devices with their start and end apart: 1, of which 1 were waited for; matrix products, arithmetic and copies ran while one was open for 0% of the time, Pallas kernels for 1%

profile of v1, /device:TPU:1, one launch (start us, length us, event | category | flops | bytes accessed | tf_op | source)
XLA Modules:
  0.0 90.5 jit_solution(5140387094344852146)
XLA Ops:
  0.6 0.0 copy-start
  0.6 0.7 copy-done
  1.4 0.8 pivots.1
  2.2 10.1 %all-to-all-start = ((bf16[8,32,128]{2,1,0:T(8,128)(2,1)}), bf16[8,32,128]{2,1,0:T(8,128)(2,1)S(1)}, u32[]{:S(2)}, u32[]{:S(2)}) async-start(bf16[8,32,128]{2,1,0:T(8,128)(2,1)} %pivots.1), calls=%async_computation | async-start | bytes 131072 | tf_op jit(solution)/shard_map/all_to_all | solution.py:322
  12.3 0.3 fusion
  12.7 0.0 copy-start.3
  12.7 0.0 copy-start.4
  12.7 0.0 copy-start.2
  12.7 0.1 pad_maximum_fusion
  12.8 0.0 copy-start.1
  12.8 0.6 copy-done.3
  13.4 0.3 index.1.place_ref
  13.7 0.0 copy-done.4
  13.8 0.0 copy-done.1
  13.8 0.1 prepare.1.kv_ref
  13.9 0.0 copy-done.2
  13.9 0.2 queries.1
  14.1 3.1 %all-to-all-done.piv_ref = bf16[8,32,128]{2,1,0:T(8,128)(2,1)S(1)} async-done(((bf16[8,32,128]{2,1,0:T(8,128)(2,1)}), bf16[8,32,128]{2,1,0:T(8,128)(2,1)S(1)}, u32[]{:S(2)}, u32[]{:S(2)}) %all-to-all-start) | async-done | bytes 65568 | tf_op jit(solution)/shard_map/all_to_all | solution.py:322
  17.2 0.5 sums.1
  17.7 11.3 %all_to_all.20.in_ref = bf16[16,48,128]{2,1,0:T(8,128)(2,1)S(1)} all-to-all(bf16[16,48,128]{2,1,0:T(8,128)(2,1)S(1)} %get-tuple-element.24), channel_id=1, replica_groups=mesh['x'=4,'far'=4,'near'=4,'head'=8] {'x','near'}, dimensions={0} | all-to-all | bytes 393216 | tf_op jit(solution)/shard_map/all_to_all | solution.py:345
  29.0 0.1 middle.1
  29.0 27.6 %all_to_all.21 = bf16[4,288,128]{2,1,0:T(8,128)(2,1)S(1)} all-to-all(bf16[4,288,128]{2,1,0:T(8,128)(2,1)S(1)} %middle.1), channel_id=1, replica_groups=mesh['x'=4,'far'=4,'near'=4,'head'=8] {'far'}, dimensions={0} | all-to-all | bytes 589824 | tf_op jit(solution)/shard_map/all_to_all | solution.py:347
  56.7 0.8 pick.1
  57.5 26.1 %all_to_all.22.in_ref = bf16[16,144,128]{2,1,0:T(8,128)(2,1)S(1)} all-to-all(bf16[16,144,128]{2,1,0:T(8,128)(2,1)S(1)} %pick.1), channel_id=1, replica_groups=mesh['x'=4,'far'=4,'near'=4,'head'=8] {'x','near'}, dimensions={0} | all-to-all | bytes 1179648 | tf_op jit(solution)/shard_map/all_to_all | solution.py:352
  83.6 6.9 %finish.1 = (bf16[128,1024]{1,0:T(8,128)(2,1)}, f32[160,128]{1,0:T(8,128)}, f32[160,128]{1,0:T(8,128)}) custom-call(s32[1]{0:T(128)} %bitcast.2.head_ref, bf16[128,1024]{1,0:T(8,128)(2,1)S(1)} %get-tuple-element.19.queries_ref, f32[128,1024]{1,0:T(8,128)S(1)} %get-tuple-element.20.bias_ref, bf16[16,144,128]{2,1,0:T(8,128)(2,1)S(1)} %all_to_all.22.in_ref, ...), custom_call_target="tpu_custom_call" | custom-call | tf_op jit(solution)/shard_map/finish/pallas_call | solution.py:312
  (2 shorter events, 0.0 us)
Async XLA Ops:
  0.6 0.8 copy-start
  2.2 15.0 %all-to-all-start = ((bf16[8,32,128]{2,1,0:T(8,128)(2,1)}), bf16[8,32,128]{2,1,0:T(8,128)(2,1)S(1)}, u32[]{:S(2)}, u32[]{:S(2)}) async-start(bf16[8,32,128]{2,1,0:T(8,128)(2,1)} %pivots.1), calls=%async_computation | async-start | bytes 131072 | tf_op jit(solution)/shard_map/all_to_all | solution.py:322
  12.7 0.8 copy-start.3
  12.7 1.1 %copy-start.4 = (bf16[128,128]{1,0:T(8,128)(2,1)S(1)}, bf16[128,128]{1,0:T(8,128)(2,1)}, u32[]{:S(2)}) copy-start(bf16[128,128]{1,0:T(8,128)(2,1)} %values_ref.1) | copy-start | bytes 98308
  12.7 1.2 %copy-start.2 = (bf16[128,1024]{1,0:T(8,128)(2,1)S(1)}, bf16[128,1024]{1,0:T(8,128)(2,1)}, u32[]{:S(2)}) copy-start(bf16[128,1024]{1,0:T(8,128)(2,1)} %queries_ref.1) | copy-start | bytes 786436
  12.8 1.0 %copy-start.1 = (bf16[128,128]{1,0:T(8,128)(2,1)S(1)}, bf16[128,128]{1,0:T(8,128)(2,1)}, u32[]{:S(2)}) copy-start(bf16[128,128]{1,0:T(8,128)(2,1)} %keys_ref.5) | copy-start | bytes 98308

commit v2 on v1

--- a/solution.py
+++ b/solution.py
@@ -214,6 +214,14 @@
         sums_ref[source * UNIT:(source + 1) * UNIT, :] = one_term(in_ref[source, SLOTS * PIECE:])
     unfold(head, 1.0 / tokens, sums_ref, work_ref)
     work_ref[:, 384:512] = pivt_ref[...].astype(jnp.float32)
+    gram = work_ref[:, 0:256]
+    row, lane = iota(gram.shape, 0), iota(gram.shape, 1)
+    diagonal = jnp.where(row == lane, gram, 0.0)
+    down = lax.rsqrt(jnp.sum(diagonal, axis=1, keepdims=True))
+    along = jnp.sum(diagonal, axis=0, keepdims=True)
+    along = lax.rsqrt(jnp.where(lane[0:1, :] < rank, along, 1.0))
+    work_ref[:, 0:256] = gram * down * along
+    work_ref[:, 256:512] = work_ref[:, 256:512] * down
     for first in range(0, rank, PANEL):
         block = work_ref[first:first + PANEL, :]
         for start in range(first, first + PANEL, STRIP):
@@ -222,14 +230,29 @@
                 jnp.broadcast_to(block[:, at:at + 1], (height, 128))
                 for at in range(start, start + STRIP)
             ]
-            for step in range(STRIP):
-                root = lax.rsqrt(columns[step][step:step + 1, :])
-                column = columns[step] * root
-                for later in range(step + 1, STRIP):
-                    columns[later] = columns[later] - column * column[later:later + 1, :]
-                line = block[step:step + 1, :] * jnp.concatenate([root] * 4, axis=1)
-                work_ref[start + step:start + step + 1, :] = line
-                block = block - jnp.concatenate([column] * 4, axis=1) * line
+            for step in range(0, STRIP, 2):
+                left, right = columns[step], columns[step + 1]
+                a, b = left[step:step + 1, :], left[step + 1:step + 2, :]
+                c = right[step + 1:step + 2, :]
+                root = lax.rsqrt(a)
+                second = a * root * lax.rsqrt(a * c - b * b)
+                mixed = b * root * root * second
+                right = right * second - left * mixed
+                left = left * root
+                for later in range(step + 2, STRIP):
+                    columns[later] = (
+                        columns[later] - left * left[later:later + 1, :]
+                    ) - right * right[later:later + 1, :]
+                root, second, mixed = (jnp.concatenate([v] * 4, axis=1) for v in (root, second, mixed))
+                upper, lower = block[step:step + 1, :], block[step + 1:step + 2, :]
+                lower = lower * second - upper * mixed
+                upper = upper * root
+                at = start + step
+                work_ref[at:at + 1, :] = upper
+                work_ref[at + 1:at + 2, :] = lower
+                block = (block - jnp.concatenate([left] * 4, axis=1) * upper) - (
+                    jnp.concatenate([right] * 4, axis=1) * lower
+                )
                 yield
             block = block[STRIP:, :]
         last = first + PANEL
@@ -282,11 +305,13 @@
         tokens, head_ref[0], in_ref, pivt_ref, factor_ref, coeffs_ref, work_ref, sums_ref
     )
     attend = attend_steps(queries_ref, bias_ref, in_ref, kv_ref, out_ref)
-    steps = pivt_ref.shape[0]
+    steps = pivt_ref.shape[0] // 2
+    given = 0
     for step in range(steps):
         next(basis, None)
-        if step % (steps // (4 * GQ)) == 0:
+        while given * steps < step * 4 * GQ:
             next(attend, None)
+            given += 1
     for rest in (attend, basis):
         for _ in rest:
             pass

time: 90.8 us -> 91.1 us (level)
  no operation moved by 1% of the time
where the time goes in v2:
time: 91.1 us; the launch traced here: 90.7 us
  blocking collectives  65 us (71%)
  starting transfers between devices  10.1 us (11%)
  Pallas kernels  9.89 us (11%)
  waiting for transfers between devices  3.06 us (3%)
  local copies, waits for them, and re-layouts  1.38 us (2%)
    all_to_all x1, blocking collectives, on_device(): second = lax.all_to_all(second, 'far', 0, 0)  27.6 us
    all_to_all x1, blocking collectives, on_device(): third = lax.all_to_all(third, near_axes, 0, 0)  26.1 us
    all_to_all x1, blocking collectives, on_device(): first = lax.all_to_all(first, near_axes, 0, 0)  11.3 us
    all_to_all x1, starting transfers between devices, on_device(): pivots = lax.all_to_all(pivots, 'head', 0, 0)  10.1 us
    pallas_call x8, Pallas kernels, call(): pl.pallas_call(kernel, out_shape=out_shape, in_specs=[smem] * scalars + [...  9.89 us
    all_to_all x1, waiting for transfers between devices, on_device(): pivots = lax.all_to_all(pivots, 'head', 0, 0)  3.06 us
  transfers between devices with their start and end apart: 1, of which 1 were waited for; matrix products, arithmetic and copies ran while one was open for 0% of the time, Pallas kernels for 1%

profile of v2, /device:TPU:1, one launch (start us, length us, event | category | flops | bytes accessed | tf_op | source)
XLA Modules:
  0.0 90.7 jit_solution(16979476610840887971)
XLA Ops:
  0.6 0.0 copy-start
  0.6 0.7 copy-done
  1.4 0.8 pivots.1
  2.2 10.1 %all-to-all-start = ((bf16[8,32,128]{2,1,0:T(8,128)(2,1)}), bf16[8,32,128]{2,1,0:T(8,128)(2,1)S(1)}, u32[]{:S(2)}, u32[]{:S(2)}) async-start(bf16[8,32,128]{2,1,0:T(8,128)(2,1)} %pivots.1), calls=%async_computation | async-start | bytes 131072 | tf_op jit(solution)/shard_map/all_to_all | solution.py:347
  12.3 0.3 fusion
  12.7 0.0 copy-start.3
  12.7 0.0 copy-start.4
  12.7 0.0 copy-start.2
  12.7 0.1 pad_maximum_fusion
  12.8 0.0 copy-start.1
  12.8 0.6 copy-done.3
  13.4 0.3 index.1.place_ref
  13.7 0.0 copy-done.4
  13.8 0.0 copy-done.1
  13.8 0.1 prepare.1.kv_ref
  13.9 0.0 copy-done.2
  13.9 0.2 queries.1
  14.1 3.1 %all-to-all-done.piv_ref = bf16[8,32,128]{2,1,0:T(8,128)(2,1)S(1)} async-done(((bf16[8,32,128]{2,1,0:T(8,128)(2,1)}), bf16[8,32,128]{2,1,0:T(8,128)(2,1)S(1)}, u32[]{:S(2)}, u32[]{:S(2)}) %all-to-all-start) | async-done | bytes 65568 | tf_op jit(solution)/shard_map/all_to_all | solution.py:347
  17.2 0.5 sums.1
  17.7 11.3 %all_to_all.20.in_ref = bf16[16,48,128]{2,1,0:T(8,128)(2,1)S(1)} all-to-all(bf16[16,48,128]{2,1,0:T(8,128)(2,1)S(1)} %get-tuple-element.24), channel_id=1, replica_groups=mesh['x'=4,'far'=4,'near'=4,'head'=8] {'x','near'}, dimensions={0} | all-to-all | bytes 393216 | tf_op jit(solution)/shard_map/all_to_all | solution.py:370
  29.0 0.1 middle.1
  29.0 27.6 %all_to_all.21 = bf16[4,288,128]{2,1,0:T(8,128)(2,1)S(1)} all-to-all(bf16[4,288,128]{2,1,0:T(8,128)(2,1)S(1)} %middle.1), channel_id=1, replica_groups=mesh['x'=4,'far'=4,'near'=4,'head'=8] {'far'}, dimensions={0} | all-to-all | bytes 589824 | tf_op jit(solution)/shard_map/all_to_all | solution.py:372
  56.7 0.8 pick.1
  57.5 26.1 %all_to_all.22.in_ref = bf16[16,144,128]{2,1,0:T(8,128)(2,1)S(1)} all-to-all(bf16[16,144,128]{2,1,0:T(8,128)(2,1)S(1)} %pick.1), channel_id=1, replica_groups=mesh['x'=4,'far'=4,'near'=4,'head'=8] {'x','near'}, dimensions={0} | all-to-all | bytes 1179648 | tf_op jit(solution)/shard_map/all_to_all | solution.py:377
  83.6 7.1 %finish.1 = (bf16[128,1024]{1,0:T(8,128)(2,1)}, f32[160,128]{1,0:T(8,128)}, f32[160,128]{1,0:T(8,128)}) custom-call(s32[1]{0:T(128)} %bitcast.2.head_ref, bf16[128,1024]{1,0:T(8,128)(2,1)S(1)} %get-tuple-element.19.queries_ref, f32[128,1024]{1,0:T(8,128)S(1)} %get-tuple-element.20.bias_ref, bf16[16,144,128]{2,1,0:T(8,128)(2,1)S(1)} %all_to_all.22.in_ref, ...), custom_call_target="tpu_custom_call" | custom-call | tf_op jit(solution)/shard_map/finish/pallas_call | solution.py:337
  (2 shorter events, 0.0 us)
Async XLA Ops:
  0.6 0.8 copy-start
  2.2 15.0 %all-to-all-start = ((bf16[8,32,128]{2,1,0:T(8,128)(2,1)}), bf16[8,32,128]{2,1,0:T(8,128)(2,1)S(1)}, u32[]{:S(2)}, u32[]{:S(2)}) async-start(bf16[8,32,128]{2,1,0:T(8,128)(2,1)} %pivots.1), calls=%async_computation | async-start | bytes 131072 | tf_op jit(solution)/shard_map/all_to_all | solution.py:347
  12.7 0.8 copy-start.3
  12.7 1.1 %copy-start.4 = (bf16[128,128]{1,0:T(8,128)(2,1)S(1)}, bf16[128,128]{1,0:T(8,128)(2,1)}, u32[]{:S(2)}) copy-start(bf16[128,128]{1,0:T(8,128)(2,1)} %values_ref.1) | copy-start | bytes 98308
  12.7 1.2 %copy-start.2 = (bf16[128,1024]{1,0:T(8,128)(2,1)S(1)}, bf16[128,1024]{1,0:T(8,128)(2,1)}, u32[]{:S(2)}) copy-start(bf16[128,1024]{1,0:T(8,128)(2,1)} %queries_ref.1) | copy-start | bytes 786436
  12.8 1.0 %copy-start.1 = (bf16[128,128]{1,0:T(8,128)(2,1)S(1)}, bf16[128,128]{1,0:T(8,128)(2,1)}, u32[]{:S(2)}) copy-start(bf16[128,128]{1,0:T(8,128)(2,1)} %keys_ref.5) | copy-start | bytes 98308

commit v3 on v1

--- a/solution.py
+++ b/solution.py
@@ -16,6 +16,7 @@
 FAR = 4
 PANEL = 40
 STRIP = 8
+TOGETHER = 2
 PIECE = 16
 UNIT = 16
 SLOTS = 7
@@ -68,7 +69,7 @@
     for g in range(GQ):
         lanes = slice(g * HD, (g + 1) * HD)
         query = turn(queries_ref[:, lanes].astype(jnp.float32), cosine, sine)
-        out_ref[:, lanes] = query.astype(jnp.bfloat16)
+        out_ref[g * TILE:(g + 1) * TILE, :] = query.astype(jnp.bfloat16)
     mask = mask_ref[0]
     count = jnp.sum(jnp.where(iota(mask.shape, 0) == me_ref[0], mask, 0)) - 1
     width = SLOTS * TILE
@@ -236,7 +237,7 @@
         if last < rank:
             done = work_ref[first:last, :]
             update = lax.dot_general(
-                done[:, 0:256], done, (((0,), (0,)), ((), ())),
+                done[:, 0:rank], done, (((0,), (0,)), ((), ())),
                 precision=lax.Precision.HIGHEST, preferred_element_type=jnp.float32,
             )
             work_ref[last:rank, :] = work_ref[last:rank, :] - update[last:rank, :]
@@ -255,12 +256,12 @@
         [in_ref[half:, 0:per_dest].reshape(width, HD), kv_ref[TILE:, :]], axis=0
     )
     scale = HD ** (-0.5) * math.log2(math.e)
-    for g in range(GQ):
-        lanes = slice(g * HD, (g + 1) * HD)
+    bias = jnp.concatenate([bias_ref[...]] * TOGETHER, axis=0)
+    for first in range(0, GQ, TOGETHER):
         scores = lax.dot_general(
-            queries_ref[:, lanes], keys, (((1,), (1,)), ((), ())),
-            preferred_element_type=jnp.float32,
-        ) * scale + bias_ref[...]
+            queries_ref[first * TILE:(first + TOGETHER) * TILE, :], keys,
+            (((1,), (1,)), ((), ())), preferred_element_type=jnp.float32,
+        ) * scale + bias
         yield
         most = jnp.max(scores, axis=1, keepdims=True)
         yield
@@ -271,7 +272,10 @@
             weights.astype(jnp.bfloat16), values, preferred_element_type=jnp.float32
         )
         yield
-        out_ref[:, lanes] = (mixed / totals).astype(jnp.bfloat16)
+        mixed = (mixed / totals).astype(jnp.bfloat16)
+        for g in range(TOGETHER):
+            lanes = slice((first + g) * HD, (first + g + 1) * HD)
+            out_ref[:, lanes] = mixed[g * TILE:(g + 1) * TILE]
 
 
 def finish_kernel(
@@ -285,7 +289,7 @@
     steps = pivt_ref.shape[0]
     for step in range(steps):
         next(basis, None)
-        if step % (steps // (4 * GQ)) == 0:
+        if step % (steps // (4 * GQ // TOGETHER)) == 0:
             next(attend, None)
     for rest in (attend, basis):
         for _ in rest:
@@ -330,7 +334,7 @@
     )
     turned, bias = call(
         queries_kernel, "queries",
-        (shape(queries.shape, bf16), shape((TILE, (SLOTS + 1) * TILE), f32)), 1,
+        (shape((GQ * TILE, HD), bf16), shape((TILE, (SLOTS + 1) * TILE), f32)), 1,
         ctx_index.reshape(1), tile_mask, queries, cosine, sine,
     )
     pivots, kv, places, turned, bias, head_index = lax.optimization_barrier(

time: 90.8 us -> 90.4 us (level)
  no operation moved by 1% of the time
where the time goes in v3:
time: 90.4 us; the launch traced here: 90 us
  blocking collectives  65 us (72%)
  starting transfers between devices  10.1 us (11%)
  Pallas kernels  9.18 us (10%)
  waiting for transfers between devices  3.07 us (3%)
  local copies, waits for them, and re-layouts  1.38 us (2%)
    all_to_all x1, blocking collectives, on_device(): second = lax.all_to_all(second, 'far', 0, 0)  27.6 us
    all_to_all x1, blocking collectives, on_device(): third = lax.all_to_all(third, near_axes, 0, 0)  26.1 us
    all_to_all x1, blocking collectives, on_device(): first = lax.all_to_all(first, near_axes, 0, 0)  11.3 us
    all_to_all x1, starting transfers between devices, on_device(): pivots = lax.all_to_all(pivots, 'head', 0, 0)  10.1 us
    pallas_call x8, Pallas kernels, call(): pl.pallas_call(kernel, out_shape=out_shape, in_specs=[smem] * scalars + [...  9.18 us
    all_to_all x1, waiting for transfers between devices, on_device(): pivots = lax.all_to_all(pivots, 'head', 0, 0)  3.07 us
  transfers between devices with their start and end apart: 1, of which 1 were waited for; matrix products, arithmetic and copies ran while one was open for 0% of the time, Pallas kernels for 1%

profile of v3, /device:TPU:1, one launch (start us, length us, event | category | flops | bytes accessed | tf_op | source)
XLA Modules:
  0.0 90.0 jit_solution(2076123761402336146)
XLA Ops:
  0.6 0.0 copy-start
  0.6 0.7 copy-done
  1.4 0.8 pivots.1
  2.2 10.1 %all-to-all-start = ((bf16[8,32,128]{2,1,0:T(8,128)(2,1)}), bf16[8,32,128]{2,1,0:T(8,128)(2,1)S(1)}, u32[]{:S(2)}, u32[]{:S(2)}) async-start(bf16[8,32,128]{2,1,0:T(8,128)(2,1)} %pivots.1), calls=%async_computation | async-start | bytes 131072 | tf_op jit(solution)/shard_map/all_to_all | solution.py:326
  12.3 0.3 fusion
  12.7 0.0 copy-start.3
  12.7 0.0 copy-start.4
  12.7 0.0 copy-start.2
  12.7 0.1 pad_maximum_fusion
  12.8 0.0 copy-start.1
  12.8 0.6 copy-done.3
  13.4 0.3 index.1.place_ref
  13.7 0.0 copy-done.4
  13.8 0.0 copy-done.1
  13.8 0.1 prepare.1.kv_ref
  13.9 0.0 copy-done.2
  13.9 0.2 queries.1
  14.1 3.1 %all-to-all-done.piv_ref = bf16[8,32,128]{2,1,0:T(8,128)(2,1)S(1)} async-done(((bf16[8,32,128]{2,1,0:T(8,128)(2,1)}), bf16[8,32,128]{2,1,0:T(8,128)(2,1)S(1)}, u32[]{:S(2)}, u32[]{:S(2)}) %all-to-all-start) | async-done | bytes 65568 | tf_op jit(solution)/shard_map/all_to_all | solution.py:326
  17.2 0.5 sums.1
  17.7 11.3 %all_to_all.20.in_ref = bf16[16,48,128]{2,1,0:T(8,128)(2,1)S(1)} all-to-all(bf16[16,48,128]{2,1,0:T(8,128)(2,1)S(1)} %get-tuple-element.24), channel_id=1, replica_groups=mesh['x'=4,'far'=4,'near'=4,'head'=8] {'x','near'}, dimensions={0} | all-to-all | bytes 393216 | tf_op jit(solution)/shard_map/all_to_all | solution.py:349
  29.0 0.1 middle.1
  29.0 27.6 %all_to_all.21 = bf16[4,288,128]{2,1,0:T(8,128)(2,1)S(1)} all-to-all(bf16[4,288,128]{2,1,0:T(8,128)(2,1)S(1)} %middle.1), channel_id=1, replica_groups=mesh['x'=4,'far'=4,'near'=4,'head'=8] {'far'}, dimensions={0} | all-to-all | bytes 589824 | tf_op jit(solution)/shard_map/all_to_all | solution.py:351
  56.7 0.8 pick.1
  57.5 26.1 %all_to_all.22.in_ref = bf16[16,144,128]{2,1,0:T(8,128)(2,1)S(1)} all-to-all(bf16[16,144,128]{2,1,0:T(8,128)(2,1)S(1)} %pick.1), channel_id=1, replica_groups=mesh['x'=4,'far'=4,'near'=4,'head'=8] {'x','near'}, dimensions={0} | all-to-all | bytes 1179648 | tf_op jit(solution)/shard_map/all_to_all | solution.py:356
  83.6 6.4 %finish.1 = (bf16[128,1024]{1,0:T(8,128)(2,1)}, f32[160,128]{1,0:T(8,128)}, f32[160,128]{1,0:T(8,128)}) custom-call(s32[1]{0:T(128)} %bitcast.2.head_ref, bf16[1024,128]{1,0:T(8,128)(2,1)S(1)} %get-tuple-element.19.queries_ref, f32[128,1024]{1,0:T(8,128)S(1)} %get-tuple-element.20.bias_ref, bf16[16,144,128]{2,1,0:T(8,128)(2,1)S(1)} %all_to_all.22.in_ref, ...), custom_call_target="tpu_custom_call" | custom-call | tf_op jit(solution)/shard_map/finish/pallas_call | solution.py:316
  (2 shorter events, 0.0 us)
Async XLA Ops:
  0.6 0.8 copy-start
  2.2 15.0 %all-to-all-start = ((bf16[8,32,128]{2,1,0:T(8,128)(2,1)}), bf16[8,32,128]{2,1,0:T(8,128)(2,1)S(1)}, u32[]{:S(2)}, u32[]{:S(2)}) async-start(bf16[8,32,128]{2,1,0:T(8,128)(2,1)} %pivots.1), calls=%async_computation | async-start | bytes 131072 | tf_op jit(solution)/shard_map/all_to_all | solution.py:326
  12.7 0.8 copy-start.3
  12.7 1.1 %copy-start.4 = (bf16[128,128]{1,0:T(8,128)(2,1)S(1)}, bf16[128,128]{1,0:T(8,128)(2,1)}, u32[]{:S(2)}) copy-start(bf16[128,128]{1,0:T(8,128)(2,1)} %values_ref.1) | copy-start | bytes 98308
  12.7 1.2 %copy-start.2 = (bf16[128,1024]{1,0:T(8,128)(2,1)S(1)}, bf16[128,1024]{1,0:T(8,128)(2,1)}, u32[]{:S(2)}) copy-start(bf16[128,1024]{1,0:T(8,128)(2,1)} %queries_ref.1) | copy-start | bytes 786436
  12.8 1.0 %copy-start.1 = (bf16[128,128]{1,0:T(8,128)(2,1)S(1)}, bf16[128,128]{1,0:T(8,128)(2,1)}, u32[]{:S(2)}) copy-start(bf16[128,128]{1,0:T(8,128)(2,1)} %keys_ref.5) | copy-start | bytes 98308

commit v4 on v3

--- a/solution.py
+++ b/solution.py
@@ -165,7 +165,15 @@
     )
 
 
-def sums_kernel(piv_ref, keys_ref, kv_ref, out_ref, pivt_ref, all_ref):
+def twist(far):
+    return far // 2 * 2
+
+
+def sums_piece(index, far, ref):
+    return ref.at[pl.ds(pl.multiple_of((index ^ twist(far)) * UNIT, UNIT), UNIT), :]
+
+
+def sums_kernel(far_ref, piv_ref, keys_ref, kv_ref, out_ref, pivt_ref, all_ref):
     heads = piv_ref.shape[0]
     rank = heads * PIVOTS
     padded = piv_ref[...].reshape(heads * 32, TILE)
@@ -181,7 +189,7 @@
     fold(cross, gram, all_ref)
     for dest in range(out_ref.shape[0]):
         out_ref[dest, 0:PIECE] = kv_ref[dest * PIECE:(dest + 1) * PIECE, :]
-        out_ref[dest, PIECE:] = two_terms(all_ref[dest * UNIT:(dest + 1) * UNIT, :])
+        out_ref[dest, PIECE:] = two_terms(sums_piece(dest, far_ref[0], all_ref)[...])
 
 
 def middle_kernel(in_ref, out_ref):
@@ -209,10 +217,10 @@
         out_ref[dest, SLOTS * PIECE:] = terms
 
 
-def basis_steps(tokens, head, in_ref, pivt_ref, factor_ref, coeffs_ref, work_ref, sums_ref):
+def basis_steps(tokens, far, head, in_ref, pivt_ref, factor_ref, coeffs_ref, work_ref, sums_ref):
     rank = pivt_ref.shape[0]
     for source in range(in_ref.shape[0]):
-        sums_ref[source * UNIT:(source + 1) * UNIT, :] = one_term(in_ref[source, SLOTS * PIECE:])
+        sums_piece(source, far, sums_ref)[...] = one_term(in_ref[source, SLOTS * PIECE:])
     unfold(head, 1.0 / tokens, sums_ref, work_ref)
     work_ref[:, 384:512] = pivt_ref[...].astype(jnp.float32)
     for first in range(0, rank, PANEL):
@@ -279,11 +287,12 @@
 
 
 def finish_kernel(
-    tokens, head_ref, queries_ref, bias_ref, in_ref, kv_ref, pivt_ref,
+    tokens, far_ref, head_ref, queries_ref, bias_ref, in_ref, kv_ref, pivt_ref,
     out_ref, factor_ref, coeffs_ref, work_ref, sums_ref,
 ):
     basis = basis_steps(
-        tokens, head_ref[0], in_ref, pivt_ref, factor_ref, coeffs_ref, work_ref, sums_ref
+        tokens, far_ref[0], head_ref[0], in_ref, pivt_ref,
+        factor_ref, coeffs_ref, work_ref, sums_ref,
     )
     attend = attend_steps(queries_ref, bias_ref, in_ref, kv_ref, out_ref)
     steps = pivt_ref.shape[0]
@@ -337,18 +346,22 @@
         (shape((GQ * TILE, HD), bf16), shape((TILE, (SLOTS + 1) * TILE), f32)), 1,
         ctx_index.reshape(1), tile_mask, queries, cosine, sine,
     )
-    pivots, kv, places, turned, bias, head_index = lax.optimization_barrier(
-        (pivots, kv, places, turned, bias, lax.axis_index("head").reshape(1))
+    far_index = far_index.reshape(1)
+    pivots, kv, places, turned, bias, far_index, head_index = lax.optimization_barrier(
+        (pivots, kv, places, turned, bias, far_index, lax.axis_index("head").reshape(1))
     )
     first, pivt = call(
         sums_kernel, "sums",
-        (shape((near_size, PIECE + 2 * UNIT, HD), bf16), shape((rank, TILE), bf16)), 0,
-        pivots, keys, kv,
+        (shape((near_size, PIECE + 2 * UNIT, HD), bf16), shape((rank, TILE), bf16)), 1,
+        far_index, pivots, keys, kv,
         scratch=[pltpu.VMEM((near_size * UNIT, HD), f32)],
     )
     first = lax.all_to_all(first, near_axes, 0, 0)
     second = call(middle_kernel, "middle", shape((far_size, stride, HD), bf16), 0, first)
-    second = lax.all_to_all(second, "far", 0, 0)
+    groups = [
+        [far * NEAR + (group ^ twist(far)) for far in range(FAR)] for group in range(NEAR)
+    ]
+    second = lax.all_to_all(second, ("far", "near"), 0, 0, axis_index_groups=groups)
     third = call(
         pick_kernel, "pick", shape((near_size, SLOTS * PIECE + 2 * UNIT, HD), bf16), 1,
         places, second.reshape(far_size * stride, HD),
@@ -357,8 +370,8 @@
 
     attn_out, key_factor, coeffs = call(
         functools.partial(finish_kernel, float(token_total)), "finish",
-        (shape(queries.shape, bf16), shape((rank, HD), f32), shape((rank, TILE), f32)), 1,
-        head_index, turned, bias, third, kv, pivt,
+        (shape(queries.shape, bf16), shape((rank, HD), f32), shape((rank, TILE), f32)), 2,
+        far_index, head_index, turned, bias, third, kv, pivt,
         scratch=[pltpu.VMEM((rank, 512), f32), pltpu.VMEM((near_size * UNIT, HD), f32)],
     )
     return (attn_out, coeffs.T, key_factor)

time: 90.4 us -> 89.8 us (level)
    all_to_all x1, blocking collectives: 26.1 us -> 23.5 us  [on_device(): third = lax.all_to_all(third, near_axes, 0, 0)]
    all_to_all x1, blocking collectives: 27.6 us -> 29.7 us  [on_device(): lax.all_to_all(second, ('far', 'near'), 0, 0, axis_index_groups=groups)]
where the time goes in v4:
time: 89.8 us; the launch traced here: 89.4 us
  blocking collectives  64.5 us (72%)
  starting transfers between devices  10.1 us (11%)
  Pallas kernels  9.15 us (10%)
  waiting for transfers between devices  3.07 us (3%)
  local copies, waits for them, and re-layouts  1.38 us (2%)
    all_to_all x1, blocking collectives, on_device(): lax.all_to_all(second, ('far', 'near'), 0, 0, axis_index_groups=groups)  29.7 us
    all_to_all x1, blocking collectives, on_device(): third = lax.all_to_all(third, near_axes, 0, 0)  23.5 us
    all_to_all x1, blocking collectives, on_device(): first = lax.all_to_all(first, near_axes, 0, 0)  11.3 us
    all_to_all x1, starting transfers between devices, on_device(): pivots = lax.all_to_all(pivots, 'head', 0, 0)  10.1 us
    pallas_call x8, Pallas kernels, call(): pl.pallas_call(kernel, out_shape=out_shape, in_specs=[smem] * scalars + [...  9.15 us
    all_to_all x1, waiting for transfers between devices, on_device(): pivots = lax.all_to_all(pivots, 'head', 0, 0)  3.07 us
  transfers between devices with their start and end apart: 1, of which 1 were waited for; matrix products, arithmetic and copies ran while one was open for 0% of the time, Pallas kernels for 1%

profile of v4, /device:TPU:1, one launch (start us, length us, event | category | flops | bytes accessed | tf_op | source)
XLA Modules:
  0.0 89.4 jit_solution(15785788378448017362)
XLA Ops:
  0.6 0.0 copy-start
  0.6 0.7 copy-done
  1.4 0.8 pivots.1
  2.2 10.1 %all-to-all-start = ((bf16[8,32,128]{2,1,0:T(8,128)(2,1)}), bf16[8,32,128]{2,1,0:T(8,128)(2,1)S(1)}, u32[]{:S(2)}, u32[]{:S(2)}) async-start(bf16[8,32,128]{2,1,0:T(8,128)(2,1)} %pivots.1), calls=%async_computation | async-start | bytes 131072 | tf_op jit(solution)/shard_map/all_to_all | solution.py:335
  12.3 0.3 fusion
  12.7 0.0 copy-start.3
  12.7 0.0 copy-start.4
  12.7 0.0 copy-start.2
  12.7 0.1 pad_maximum_fusion
  12.8 0.0 copy-start.1
  12.8 0.6 copy-done.3
  13.4 0.3 index.1.place_ref
  13.7 0.0 copy-done.4
  13.8 0.0 copy-done.1
  13.8 0.1 prepare.1.kv_ref
  13.9 0.0 copy-done.2
  13.9 0.2 queries.1
  14.1 3.1 %all-to-all-done.piv_ref = bf16[8,32,128]{2,1,0:T(8,128)(2,1)S(1)} async-done(((bf16[8,32,128]{2,1,0:T(8,128)(2,1)}), bf16[8,32,128]{2,1,0:T(8,128)(2,1)S(1)}, u32[]{:S(2)}, u32[]{:S(2)}) %all-to-all-start) | async-done | bytes 65568 | tf_op jit(solution)/shard_map/all_to_all | solution.py:335
  17.2 0.5 sums.1
  17.7 11.3 %all_to_all.20.in_ref = bf16[16,48,128]{2,1,0:T(8,128)(2,1)S(1)} all-to-all(bf16[16,48,128]{2,1,0:T(8,128)(2,1)S(1)} %get-tuple-element.26), channel_id=1, replica_groups=mesh['x'=4,'far'=4,'near'=4,'head'=8] {'x','near'}, dimensions={0} | all-to-all | bytes 393216 | tf_op jit(solution)/shard_map/all_to_all | solution.py:359
  29.0 0.1 middle.1
  29.1 29.7 %all_to_all.21 = bf16[4,288,128]{2,1,0:T(8,128)(2,1)S(1)} all-to-all(bf16[4,288,128]{2,1,0:T(8,128)(2,1)S(1)} %middle.1), channel_id=1, replica_groups={{0,32,80,112},{8,40,88,120},{16,48,64,96},{24,56,72,104},{1,33,81,113},..., dimensions={0} | all-to-all | bytes 589824 | tf_op jit(solution)/shard_map/all_to_all | solution.py:364
  58.7 0.8 pick.1
  59.5 23.5 %all_to_all.22.in_ref = bf16[16,144,128]{2,1,0:T(8,128)(2,1)S(1)} all-to-all(bf16[16,144,128]{2,1,0:T(8,128)(2,1)S(1)} %pick.1), channel_id=1, replica_groups=mesh['x'=4,'far'=4,'near'=4,'head'=8] {'x','near'}, dimensions={0} | all-to-all | bytes 1179648 | tf_op jit(solution)/shard_map/all_to_all | solution.py:369
  83.1 6.4 %finish.1 = (bf16[128,1024]{1,0:T(8,128)(2,1)}, f32[160,128]{1,0:T(8,128)}, f32[160,128]{1,0:T(8,128)}) custom-call(s32[1]{0:T(128)} %bitcast.far_ref, s32[1]{0:T(128)} %bitcast.2.head_ref, bf16[1024,128]{1,0:T(8,128)(2,1)S(1)} %get-tuple-element.21.queries_ref, f32[128,1024]{1,0:T(8,128)S(1)} %get-tuple-element.22.bias_ref, ...), custom_call_target="tpu_custom_call" | custom-call | tf_op jit(solution)/shard_map/finish/pallas_call | solution.py:325
  (2 shorter events, 0.0 us)
Async XLA Ops:
  0.6 0.8 copy-start
  2.2 15.0 %all-to-all-start = ((bf16[8,32,128]{2,1,0:T(8,128)(2,1)}), bf16[8,32,128]{2,1,0:T(8,128)(2,1)S(1)}, u32[]{:S(2)}, u32[]{:S(2)}) async-start(bf16[8,32,128]{2,1,0:T(8,128)(2,1)} %pivots.1), calls=%async_computation | async-start | bytes 131072 | tf_op jit(solution)/shard_map/all_to_all | solution.py:335
  12.7 0.8 copy-start.3
  12.7 1.1 %copy-start.4 = (bf16[128,128]{1,0:T(8,128)(2,1)S(1)}, bf16[128,128]{1,0:T(8,128)(2,1)}, u32[]{:S(2)}) copy-start(bf16[128,128]{1,0:T(8,128)(2,1)} %values_ref.1) | copy-start | bytes 98308
  12.7 1.2 %copy-start.2 = (bf16[128,1024]{1,0:T(8,128)(2,1)S(1)}, bf16[128,1024]{1,0:T(8,128)(2,1)}, u32[]{:S(2)}) copy-start(bf16[128,1024]{1,0:T(8,128)(2,1)} %queries_ref.1) | copy-start | bytes 786436
  12.8 1.0 %copy-start.1 = (bf16[128,128]{1,0:T(8,128)(2,1)S(1)}, bf16[128,128]{1,0:T(8,128)(2,1)}, u32[]{:S(2)}) copy-start(bf16[128,128]{1,0:T(8,128)(2,1)} %keys_ref.5) | copy-start | bytes 98308

commit v5 on v4

--- a/solution.py
+++ b/solution.py
@@ -14,9 +14,9 @@
 PIVOTS = 20
 NEAR = 4
 FAR = 4
-PANEL = 40
+PANEL = 32
 STRIP = 8
-TOGETHER = 2
+TOGETHER = 4
 PIECE = 16
 UNIT = 16
 SLOTS = 7

time: 89.8 us -> 89.9 us (level)
  no operation moved by 1% of the time
where the time goes in v5:
time: 89.9 us; the launch traced here: 89.6 us
  blocking collectives  64.5 us (72%)
  starting transfers between devices  10.1 us (11%)
  Pallas kernels  9.27 us (10%)
  waiting for transfers between devices  3.07 us (3%)
  local copies, waits for them, and re-layouts  1.38 us (2%)
    all_to_all x1, blocking collectives, on_device(): lax.all_to_all(second, ('far', 'near'), 0, 0, axis_index_groups=groups)  29.7 us
    all_to_all x1, blocking collectives, on_device(): third = lax.all_to_all(third, near_axes, 0, 0)  23.5 us
    all_to_all x1, blocking collectives, on_device(): first = lax.all_to_all(first, near_axes, 0, 0)  11.3 us
    all_to_all x1, starting transfers between devices, on_device(): pivots = lax.all_to_all(pivots, 'head', 0, 0)  10.1 us
    pallas_call x8, Pallas kernels, call(): pl.pallas_call(kernel, out_shape=out_shape, in_specs=[smem] * scalars + [...  9.27 us
    all_to_all x1, waiting for transfers between devices, on_device(): pivots = lax.all_to_all(pivots, 'head', 0, 0)  3.07 us
  transfers between devices with their start and end apart: 1, of which 1 were waited for; matrix products, arithmetic and copies ran while one was open for 0% of the time, Pallas kernels for 1%

profile of v5, /device:TPU:1, one launch (start us, length us, event | category | flops | bytes accessed | tf_op | source)
XLA Modules:
  0.0 89.6 jit_solution(16621641065022124261)
XLA Ops:
  0.6 0.0 copy-start
  0.6 0.7 copy-done
  1.4 0.8 pivots.1
  2.2 10.1 %all-to-all-start = ((bf16[8,32,128]{2,1,0:T(8,128)(2,1)}), bf16[8,32,128]{2,1,0:T(8,128)(2,1)S(1)}, u32[]{:S(2)}, u32[]{:S(2)}) async-start(bf16[8,32,128]{2,1,0:T(8,128)(2,1)} %pivots.1), calls=%async_computation | async-start | bytes 131072 | tf_op jit(solution)/shard_map/all_to_all | solution.py:335
  12.3 0.3 fusion
  12.7 0.0 copy-start.3
  12.7 0.0 copy-start.4
  12.7 0.0 copy-start.2
  12.7 0.1 pad_maximum_fusion
  12.8 0.0 copy-start.1
  12.8 0.6 copy-done.3
  13.4 0.3 index.1.place_ref
  13.7 0.0 copy-done.4
  13.8 0.0 copy-done.1
  13.8 0.1 prepare.1.kv_ref
  13.9 0.0 copy-done.2
  13.9 0.2 queries.1
  14.1 3.1 %all-to-all-done.piv_ref = bf16[8,32,128]{2,1,0:T(8,128)(2,1)S(1)} async-done(((bf16[8,32,128]{2,1,0:T(8,128)(2,1)}), bf16[8,32,128]{2,1,0:T(8,128)(2,1)S(1)}, u32[]{:S(2)}, u32[]{:S(2)}) %all-to-all-start) | async-done | bytes 65568 | tf_op jit(solution)/shard_map/all_to_all | solution.py:335
  17.2 0.5 sums.1
  17.7 11.3 %all_to_all.20.in_ref = bf16[16,48,128]{2,1,0:T(8,128)(2,1)S(1)} all-to-all(bf16[16,48,128]{2,1,0:T(8,128)(2,1)S(1)} %get-tuple-element.26), channel_id=1, replica_groups=mesh['x'=4,'far'=4,'near'=4,'head'=8] {'x','near'}, dimensions={0} | all-to-all | bytes 393216 | tf_op jit(solution)/shard_map/all_to_all | solution.py:359
  29.0 0.1 middle.1
  29.1 29.7 %all_to_all.21 = bf16[4,288,128]{2,1,0:T(8,128)(2,1)S(1)} all-to-all(bf16[4,288,128]{2,1,0:T(8,128)(2,1)S(1)} %middle.1), channel_id=1, replica_groups={{0,32,80,112},{8,40,88,120},{16,48,64,96},{24,56,72,104},{1,33,81,113},..., dimensions={0} | all-to-all | bytes 589824 | tf_op jit(solution)/shard_map/all_to_all | solution.py:364
  58.7 0.8 pick.1
  59.5 23.5 %all_to_all.22.in_ref = bf16[16,144,128]{2,1,0:T(8,128)(2,1)S(1)} all-to-all(bf16[16,144,128]{2,1,0:T(8,128)(2,1)S(1)} %pick.1), channel_id=1, replica_groups=mesh['x'=4,'far'=4,'near'=4,'head'=8] {'x','near'}, dimensions={0} | all-to-all | bytes 1179648 | tf_op jit(solution)/shard_map/all_to_all | solution.py:369
  83.1 6.5 %finish.1 = (bf16[128,1024]{1,0:T(8,128)(2,1)}, f32[160,128]{1,0:T(8,128)}, f32[160,128]{1,0:T(8,128)}) custom-call(s32[1]{0:T(128)} %bitcast.far_ref, s32[1]{0:T(128)} %bitcast.2.head_ref, bf16[1024,128]{1,0:T(8,128)(2,1)S(1)} %get-tuple-element.21.queries_ref, f32[128,1024]{1,0:T(8,128)S(1)} %get-tuple-element.22.bias_ref, ...), custom_call_target="tpu_custom_call" | custom-call | tf_op jit(solution)/shard_map/finish/pallas_call | solution.py:325
  (2 shorter events, 0.0 us)
Async XLA Ops:
  0.6 0.8 copy-start
  2.2 15.0 %all-to-all-start = ((bf16[8,32,128]{2,1,0:T(8,128)(2,1)}), bf16[8,32,128]{2,1,0:T(8,128)(2,1)S(1)}, u32[]{:S(2)}, u32[]{:S(2)}) async-start(bf16[8,32,128]{2,1,0:T(8,128)(2,1)} %pivots.1), calls=%async_computation | async-start | bytes 131072 | tf_op jit(solution)/shard_map/all_to_all | solution.py:335
  12.7 0.8 copy-start.3
  12.7 1.1 %copy-start.4 = (bf16[128,128]{1,0:T(8,128)(2,1)S(1)}, bf16[128,128]{1,0:T(8,128)(2,1)}, u32[]{:S(2)}) copy-start(bf16[128,128]{1,0:T(8,128)(2,1)} %values_ref.1) | copy-start | bytes 98308
  12.7 1.2 %copy-start.2 = (bf16[128,1024]{1,0:T(8,128)(2,1)S(1)}, bf16[128,1024]{1,0:T(8,128)(2,1)}, u32[]{:S(2)}) copy-start(bf16[128,1024]{1,0:T(8,128)(2,1)} %queries_ref.1) | copy-start | bytes 786436
  12.8 1.0 %copy-start.1 = (bf16[128,128]{1,0:T(8,128)(2,1)S(1)}, bf16[128,128]{1,0:T(8,128)(2,1)}, u32[]{:S(2)}) copy-start(bf16[128,128]{1,0:T(8,128)(2,1)} %keys_ref.5) | copy-start | bytes 98308

commit v6 on v4

--- a/solution.py
+++ b/solution.py
@@ -14,7 +14,7 @@
 PIVOTS = 20
 NEAR = 4
 FAR = 4
-PANEL = 40
+PANEL = 80
 STRIP = 8
 TOGETHER = 2
 PIECE = 16

time: 89.8 us -> 89.7 us (level)
  no operation moved by 1% of the time
where the time goes in v6:
time: 89.7 us; the launch traced here: 89.3 us
  blocking collectives  64.5 us (72%)
  starting transfers between devices  10.1 us (11%)
  Pallas kernels  9.01 us (10%)
  waiting for transfers between devices  3.07 us (3%)
  local copies, waits for them, and re-layouts  1.38 us (2%)
    all_to_all x1, blocking collectives, on_device(): lax.all_to_all(second, ('far', 'near'), 0, 0, axis_index_groups=groups)  29.7 us
    all_to_all x1, blocking collectives, on_device(): third = lax.all_to_all(third, near_axes, 0, 0)  23.5 us
    all_to_all x1, blocking collectives, on_device(): first = lax.all_to_all(first, near_axes, 0, 0)  11.3 us
    all_to_all x1, starting transfers between devices, on_device(): pivots = lax.all_to_all(pivots, 'head', 0, 0)  10.1 us
    pallas_call x8, Pallas kernels, call(): pl.pallas_call(kernel, out_shape=out_shape, in_specs=[smem] * scalars + [...  9.01 us
    all_to_all x1, waiting for transfers between devices, on_device(): pivots = lax.all_to_all(pivots, 'head', 0, 0)  3.07 us
  transfers between devices with their start and end apart: 1, of which 1 were waited for; matrix products, arithmetic and copies ran while one was open for 0% of the time, Pallas kernels for 1%

profile of v6, /device:TPU:1, one launch (start us, length us, event | category | flops | bytes accessed | tf_op | source)
XLA Modules:
  0.0 89.3 jit_solution(4381237798143445146)
XLA Ops:
  0.6 0.0 copy-start
  0.6 0.7 copy-done
  1.4 0.8 pivots.1
  2.2 10.1 %all-to-all-start = ((bf16[8,32,128]{2,1,0:T(8,128)(2,1)}), bf16[8,32,128]{2,1,0:T(8,128)(2,1)S(1)}, u32[]{:S(2)}, u32[]{:S(2)}) async-start(bf16[8,32,128]{2,1,0:T(8,128)(2,1)} %pivots.1), calls=%async_computation | async-start | bytes 131072 | tf_op jit(solution)/shard_map/all_to_all | solution.py:335
  12.3 0.3 fusion
  12.7 0.0 copy-start.3
  12.7 0.0 copy-start.4
  12.7 0.0 copy-start.2
  12.7 0.1 pad_maximum_fusion
  12.8 0.0 copy-start.1
  12.8 0.6 copy-done.3
  13.4 0.3 index.1.place_ref
  13.7 0.0 copy-done.4
  13.8 0.0 copy-done.1
  13.8 0.1 prepare.1.kv_ref
  13.9 0.0 copy-done.2
  13.9 0.2 queries.1
  14.1 3.1 %all-to-all-done.piv_ref = bf16[8,32,128]{2,1,0:T(8,128)(2,1)S(1)} async-done(((bf16[8,32,128]{2,1,0:T(8,128)(2,1)}), bf16[8,32,128]{2,1,0:T(8,128)(2,1)S(1)}, u32[]{:S(2)}, u32[]{:S(2)}) %all-to-all-start) | async-done | bytes 65568 | tf_op jit(solution)/shard_map/all_to_all | solution.py:335
  17.2 0.5 sums.1
  17.7 11.3 %all_to_all.20.in_ref = bf16[16,48,128]{2,1,0:T(8,128)(2,1)S(1)} all-to-all(bf16[16,48,128]{2,1,0:T(8,128)(2,1)S(1)} %get-tuple-element.26), channel_id=1, replica_groups=mesh['x'=4,'far'=4,'near'=4,'head'=8] {'x','near'}, dimensions={0} | all-to-all | bytes 393216 | tf_op jit(solution)/shard_map/all_to_all | solution.py:359
  29.0 0.1 middle.1
  29.1 29.7 %all_to_all.21 = bf16[4,288,128]{2,1,0:T(8,128)(2,1)S(1)} all-to-all(bf16[4,288,128]{2,1,0:T(8,128)(2,1)S(1)} %middle.1), channel_id=1, replica_groups={{0,32,80,112},{8,40,88,120},{16,48,64,96},{24,56,72,104},{1,33,81,113},..., dimensions={0} | all-to-all | bytes 589824 | tf_op jit(solution)/shard_map/all_to_all | solution.py:364
  58.7 0.8 pick.1
  59.5 23.5 %all_to_all.22.in_ref = bf16[16,144,128]{2,1,0:T(8,128)(2,1)S(1)} all-to-all(bf16[16,144,128]{2,1,0:T(8,128)(2,1)S(1)} %pick.1), channel_id=1, replica_groups=mesh['x'=4,'far'=4,'near'=4,'head'=8] {'x','near'}, dimensions={0} | all-to-all | bytes 1179648 | tf_op jit(solution)/shard_map/all_to_all | solution.py:369
  83.1 6.2 %finish.1 = (bf16[128,1024]{1,0:T(8,128)(2,1)}, f32[160,128]{1,0:T(8,128)}, f32[160,128]{1,0:T(8,128)}) custom-call(s32[1]{0:T(128)} %bitcast.far_ref, s32[1]{0:T(128)} %bitcast.2.head_ref, bf16[1024,128]{1,0:T(8,128)(2,1)S(1)} %get-tuple-element.21.queries_ref, f32[128,1024]{1,0:T(8,128)S(1)} %get-tuple-element.22.bias_ref, ...), custom_call_target="tpu_custom_call" | custom-call | tf_op jit(solution)/shard_map/finish/pallas_call | solution.py:325
  (2 shorter events, 0.0 us)
Async XLA Ops:
  0.6 0.8 copy-start
  2.2 15.0 %all-to-all-start = ((bf16[8,32,128]{2,1,0:T(8,128)(2,1)}), bf16[8,32,128]{2,1,0:T(8,128)(2,1)S(1)}, u32[]{:S(2)}, u32[]{:S(2)}) async-start(bf16[8,32,128]{2,1,0:T(8,128)(2,1)} %pivots.1), calls=%async_computation | async-start | bytes 131072 | tf_op jit(solution)/shard_map/all_to_all | solution.py:335
  12.7 0.8 copy-start.3
  12.7 1.1 %copy-start.4 = (bf16[128,128]{1,0:T(8,128)(2,1)S(1)}, bf16[128,128]{1,0:T(8,128)(2,1)}, u32[]{:S(2)}) copy-start(bf16[128,128]{1,0:T(8,128)(2,1)} %values_ref.1) | copy-start | bytes 98308
  12.7 1.2 %copy-start.2 = (bf16[128,1024]{1,0:T(8,128)(2,1)S(1)}, bf16[128,1024]{1,0:T(8,128)(2,1)}, u32[]{:S(2)}) copy-start(bf16[128,1024]{1,0:T(8,128)(2,1)} %queries_ref.1) | copy-start | bytes 786436
  12.8 1.0 %copy-start.1 = (bf16[128,128]{1,0:T(8,128)(2,1)S(1)}, bf16[128,128]{1,0:T(8,128)(2,1)}, u32[]{:S(2)}) copy-start(bf16[128,128]{1,0:T(8,128)(2,1)} %keys_ref.5) | copy-start | bytes 98308

commit v7 on v4

--- a/solution.py
+++ b/solution.py
@@ -16,6 +16,7 @@
 FAR = 4
 PANEL = 40
 STRIP = 8
+AHEAD = 5
 TOGETHER = 2
 PIECE = 16
 UNIT = 16
@@ -217,6 +218,13 @@
         out_ref[dest, SLOTS * PIECE:] = terms
 
 
+def spread_columns(block, start):
+    return [
+        jnp.broadcast_to(block[:, at:at + 1], (block.shape[0], 128))
+        for at in range(start, start + STRIP)
+    ]
+
+
 def basis_steps(tokens, far, head, in_ref, pivt_ref, factor_ref, coeffs_ref, work_ref, sums_ref):
     rank = pivt_ref.shape[0]
     for source in range(in_ref.shape[0]):
@@ -226,20 +234,26 @@
     for first in range(0, rank, PANEL):
         block = work_ref[first:first + PANEL, :]
         for start in range(first, first + PANEL, STRIP):
-            height = block.shape[0]
-            columns = [
-                jnp.broadcast_to(block[:, at:at + 1], (height, 128))
-                for at in range(start, start + STRIP)
-            ]
+            following = start + STRIP < first + PANEL
+            if start == first:
+                columns = spread_columns(block, start)
             for step in range(STRIP):
+                if following and step == AHEAD:
+                    coming = spread_columns(block, start + STRIP)
                 root = lax.rsqrt(columns[step][step:step + 1, :])
                 column = columns[step] * root
                 for later in range(step + 1, STRIP):
                     columns[later] = columns[later] - column * column[later:later + 1, :]
+                if following and step >= AHEAD:
+                    for k in range(STRIP):
+                        at = STRIP + k
+                        coming[k] = coming[k] - column * column[at:at + 1, :]
                 line = block[step:step + 1, :] * jnp.concatenate([root] * 4, axis=1)
                 work_ref[start + step:start + step + 1, :] = line
                 block = block - jnp.concatenate([column] * 4, axis=1) * line
                 yield
+            if following:
+                columns = [one[STRIP:, :] for one in coming]
             block = block[STRIP:, :]
         last = first + PANEL
         if last < rank:

time: 89.8 us -> 89.5 us (level)
  no operation moved by 1% of the time
where the time goes in v7:
time: 89.5 us; the launch traced here: 89.1 us
  blocking collectives  64.5 us (72%)
  starting transfers between devices  10.1 us (11%)
  Pallas kernels  8.82 us (10%)
  waiting for transfers between devices  3.07 us (3%)
  local copies, waits for them, and re-layouts  1.38 us (2%)
    all_to_all x1, blocking collectives, on_device(): lax.all_to_all(second, ('far', 'near'), 0, 0, axis_index_groups=groups)  29.7 us
    all_to_all x1, blocking collectives, on_device(): third = lax.all_to_all(third, near_axes, 0, 0)  23.5 us
    all_to_all x1, blocking collectives, on_device(): first = lax.all_to_all(first, near_axes, 0, 0)  11.3 us
    all_to_all x1, starting transfers between devices, on_device(): pivots = lax.all_to_all(pivots, 'head', 0, 0)  10.1 us
    pallas_call x8, Pallas kernels, call(): pl.pallas_call(kernel, out_shape=out_shape, in_specs=[smem] * scalars + [...  8.82 us
    all_to_all x1, waiting for transfers between devices, on_device(): pivots = lax.all_to_all(pivots, 'head', 0, 0)  3.07 us
  transfers between devices with their start and end apart: 1, of which 1 were waited for; matrix products, arithmetic and copies ran while one was open for 0% of the time, Pallas kernels for 1%

profile of v7, /device:TPU:1, one launch (start us, length us, event | category | flops | bytes accessed | tf_op | source)
XLA Modules:
  0.0 89.1 jit_solution(2893697061808094581)
XLA Ops:
  0.6 0.0 copy-start
  0.6 0.7 copy-done
  1.4 0.8 pivots.1
  2.2 10.1 %all-to-all-start = ((bf16[8,32,128]{2,1,0:T(8,128)(2,1)}), bf16[8,32,128]{2,1,0:T(8,128)(2,1)S(1)}, u32[]{:S(2)}, u32[]{:S(2)}) async-start(bf16[8,32,128]{2,1,0:T(8,128)(2,1)} %pivots.1), calls=%async_computation | async-start | bytes 131072 | tf_op jit(solution)/shard_map/all_to_all | solution.py:349
  12.3 0.3 fusion
  12.7 0.0 copy-start.3
  12.7 0.0 copy-start.4
  12.7 0.0 copy-start.2
  12.7 0.1 pad_maximum_fusion
  12.8 0.0 copy-start.1
  12.8 0.6 copy-done.3
  13.4 0.3 index.1.place_ref
  13.7 0.0 copy-done.4
  13.8 0.0 copy-done.1
  13.8 0.1 prepare.1.kv_ref
  13.9 0.0 copy-done.2
  13.9 0.2 queries.1
  14.1 3.1 %all-to-all-done.piv_ref = bf16[8,32,128]{2,1,0:T(8,128)(2,1)S(1)} async-done(((bf16[8,32,128]{2,1,0:T(8,128)(2,1)}), bf16[8,32,128]{2,1,0:T(8,128)(2,1)S(1)}, u32[]{:S(2)}, u32[]{:S(2)}) %all-to-all-start) | async-done | bytes 65568 | tf_op jit(solution)/shard_map/all_to_all | solution.py:349
  17.2 0.5 sums.1
  17.7 11.3 %all_to_all.20.in_ref = bf16[16,48,128]{2,1,0:T(8,128)(2,1)S(1)} all-to-all(bf16[16,48,128]{2,1,0:T(8,128)(2,1)S(1)} %get-tuple-element.26), channel_id=1, replica_groups=mesh['x'=4,'far'=4,'near'=4,'head'=8] {'x','near'}, dimensions={0} | all-to-all | bytes 393216 | tf_op jit(solution)/shard_map/all_to_all | solution.py:373
  29.0 0.1 middle.1
  29.1 29.7 %all_to_all.21 = bf16[4,288,128]{2,1,0:T(8,128)(2,1)S(1)} all-to-all(bf16[4,288,128]{2,1,0:T(8,128)(2,1)S(1)} %middle.1), channel_id=1, replica_groups={{0,32,80,112},{8,40,88,120},{16,48,64,96},{24,56,72,104},{1,33,81,113},..., dimensions={0} | all-to-all | bytes 589824 | tf_op jit(solution)/shard_map/all_to_all | solution.py:378
  58.7 0.8 pick.1
  59.5 23.5 %all_to_all.22.in_ref = bf16[16,144,128]{2,1,0:T(8,128)(2,1)S(1)} all-to-all(bf16[16,144,128]{2,1,0:T(8,128)(2,1)S(1)} %pick.1), channel_id=1, replica_groups=mesh['x'=4,'far'=4,'near'=4,'head'=8] {'x','near'}, dimensions={0} | all-to-all | bytes 1179648 | tf_op jit(solution)/shard_map/all_to_all | solution.py:383
  83.1 6.0 %finish.1 = (bf16[128,1024]{1,0:T(8,128)(2,1)}, f32[160,128]{1,0:T(8,128)}, f32[160,128]{1,0:T(8,128)}) custom-call(s32[1]{0:T(128)} %bitcast.far_ref, s32[1]{0:T(128)} %bitcast.2.head_ref, bf16[1024,128]{1,0:T(8,128)(2,1)S(1)} %get-tuple-element.21.queries_ref, f32[128,1024]{1,0:T(8,128)S(1)} %get-tuple-element.22.bias_ref, ...), custom_call_target="tpu_custom_call" | custom-call | tf_op jit(solution)/shard_map/finish/pallas_call | solution.py:339
  (2 shorter events, 0.0 us)
Async XLA Ops:
  0.6 0.8 copy-start
  2.2 15.0 %all-to-all-start = ((bf16[8,32,128]{2,1,0:T(8,128)(2,1)}), bf16[8,32,128]{2,1,0:T(8,128)(2,1)S(1)}, u32[]{:S(2)}, u32[]{:S(2)}) async-start(bf16[8,32,128]{2,1,0:T(8,128)(2,1)} %pivots.1), calls=%async_computation | async-start | bytes 131072 | tf_op jit(solution)/shard_map/all_to_all | solution.py:349
  12.7 0.8 copy-start.3
  12.7 1.1 %copy-start.4 = (bf16[128,128]{1,0:T(8,128)(2,1)S(1)}, bf16[128,128]{1,0:T(8,128)(2,1)}, u32[]{:S(2)}) copy-start(bf16[128,128]{1,0:T(8,128)(2,1)} %values_ref.1) | copy-start | bytes 98308
  12.7 1.2 %copy-start.2 = (bf16[128,1024]{1,0:T(8,128)(2,1)S(1)}, bf16[128,1024]{1,0:T(8,128)(2,1)}, u32[]{:S(2)}) copy-start(bf16[128,1024]{1,0:T(8,128)(2,1)} %queries_ref.1) | copy-start | bytes 786436
  12.8 1.0 %copy-start.1 = (bf16[128,128]{1,0:T(8,128)(2,1)S(1)}, bf16[128,128]{1,0:T(8,128)(2,1)}, u32[]{:S(2)}) copy-start(bf16[128,128]{1,0:T(8,128)(2,1)} %keys_ref.5) | copy-start | bytes 98308

commit v8 on v7

--- a/solution.py
+++ b/solution.py
@@ -14,7 +14,7 @@
 PIVOTS = 20
 NEAR = 4
 FAR = 4
-PANEL = 40
+PANEL = 80
 STRIP = 8
 AHEAD = 5
 TOGETHER = 2

time: 89.5 us -> 90.1 us (level)
  no operation moved by 1% of the time
where the time goes in v8:
time: 90.1 us; the launch traced here: 89.7 us
  blocking collectives  64.5 us (72%)
  starting transfers between devices  10.1 us (11%)
  Pallas kernels  9.41 us (10%)
  waiting for transfers between devices  3.07 us (3%)
  local copies, waits for them, and re-layouts  1.38 us (2%)
    all_to_all x1, blocking collectives, on_device(): lax.all_to_all(second, ('far', 'near'), 0, 0, axis_index_groups=groups)  29.7 us
    all_to_all x1, blocking collectives, on_device(): third = lax.all_to_all(third, near_axes, 0, 0)  23.5 us
    all_to_all x1, blocking collectives, on_device(): first = lax.all_to_all(first, near_axes, 0, 0)  11.3 us
    all_to_all x1, starting transfers between devices, on_device(): pivots = lax.all_to_all(pivots, 'head', 0, 0)  10.1 us
    pallas_call x8, Pallas kernels, call(): pl.pallas_call(kernel, out_shape=out_shape, in_specs=[smem] * scalars + [...  9.41 us
    all_to_all x1, waiting for transfers between devices, on_device(): pivots = lax.all_to_all(pivots, 'head', 0, 0)  3.07 us
  transfers between devices with their start and end apart: 1, of which 1 were waited for; matrix products, arithmetic and copies ran while one was open for 0% of the time, Pallas kernels for 1%

profile of v8, /device:TPU:1, one launch (start us, length us, event | category | flops | bytes accessed | tf_op | source)
XLA Modules:
  0.0 89.7 jit_solution(11838360682477421695)
XLA Ops:
  0.6 0.0 copy-start
  0.6 0.7 copy-done
  1.4 0.8 pivots.1
  2.2 10.1 %all-to-all-start = ((bf16[8,32,128]{2,1,0:T(8,128)(2,1)}), bf16[8,32,128]{2,1,0:T(8,128)(2,1)S(1)}, u32[]{:S(2)}, u32[]{:S(2)}) async-start(bf16[8,32,128]{2,1,0:T(8,128)(2,1)} %pivots.1), calls=%async_computation | async-start | bytes 131072 | tf_op jit(solution)/shard_map/all_to_all | solution.py:349
  12.3 0.3 fusion
  12.7 0.0 copy-start.3
  12.7 0.0 copy-start.4
  12.7 0.0 copy-start.2
  12.7 0.1 pad_maximum_fusion
  12.8 0.0 copy-start.1
  12.8 0.6 copy-done.3
  13.4 0.3 index.1.place_ref
  13.7 0.0 copy-done.4
  13.8 0.0 copy-done.1
  13.8 0.1 prepare.1.kv_ref
  13.9 0.0 copy-done.2
  13.9 0.2 queries.1
  14.1 3.1 %all-to-all-done.piv_ref = bf16[8,32,128]{2,1,0:T(8,128)(2,1)S(1)} async-done(((bf16[8,32,128]{2,1,0:T(8,128)(2,1)}), bf16[8,32,128]{2,1,0:T(8,128)(2,1)S(1)}, u32[]{:S(2)}, u32[]{:S(2)}) %all-to-all-start) | async-done | bytes 65568 | tf_op jit(solution)/shard_map/all_to_all | solution.py:349
  17.2 0.5 sums.1
  17.7 11.3 %all_to_all.20.in_ref = bf16[16,48,128]{2,1,0:T(8,128)(2,1)S(1)} all-to-all(bf16[16,48,128]{2,1,0:T(8,128)(2,1)S(1)} %get-tuple-element.26), channel_id=1, replica_groups=mesh['x'=4,'far'=4,'near'=4,'head'=8] {'x','near'}, dimensions={0} | all-to-all | bytes 393216 | tf_op jit(solution)/shard_map/all_to_all | solution.py:373
  29.0 0.1 middle.1
  29.1 29.7 %all_to_all.21 = bf16[4,288,128]{2,1,0:T(8,128)(2,1)S(1)} all-to-all(bf16[4,288,128]{2,1,0:T(8,128)(2,1)S(1)} %middle.1), channel_id=1, replica_groups={{0,32,80,112},{8,40,88,120},{16,48,64,96},{24,56,72,104},{1,33,81,113},..., dimensions={0} | all-to-all | bytes 589824 | tf_op jit(solution)/shard_map/all_to_all | solution.py:378
  58.7 0.8 pick.1
  59.5 23.5 %all_to_all.22.in_ref = bf16[16,144,128]{2,1,0:T(8,128)(2,1)S(1)} all-to-all(bf16[16,144,128]{2,1,0:T(8,128)(2,1)S(1)} %pick.1), channel_id=1, replica_groups=mesh['x'=4,'far'=4,'near'=4,'head'=8] {'x','near'}, dimensions={0} | all-to-all | bytes 1179648 | tf_op jit(solution)/shard_map/all_to_all | solution.py:383
  83.1 6.6 %finish.1 = (bf16[128,1024]{1,0:T(8,128)(2,1)}, f32[160,128]{1,0:T(8,128)}, f32[160,128]{1,0:T(8,128)}) custom-call(s32[1]{0:T(128)} %bitcast.far_ref, s32[1]{0:T(128)} %bitcast.2.head_ref, bf16[1024,128]{1,0:T(8,128)(2,1)S(1)} %get-tuple-element.21.queries_ref, f32[128,1024]{1,0:T(8,128)S(1)} %get-tuple-element.22.bias_ref, ...), custom_call_target="tpu_custom_call" | custom-call | tf_op jit(solution)/shard_map/finish/pallas_call | solution.py:339
  (2 shorter events, 0.0 us)
Async XLA Ops:
  0.6 0.8 copy-start
  2.2 15.0 %all-to-all-start = ((bf16[8,32,128]{2,1,0:T(8,128)(2,1)}), bf16[8,32,128]{2,1,0:T(8,128)(2,1)S(1)}, u32[]{:S(2)}, u32[]{:S(2)}) async-start(bf16[8,32,128]{2,1,0:T(8,128)(2,1)} %pivots.1), calls=%async_computation | async-start | bytes 131072 | tf_op jit(solution)/shard_map/all_to_all | solution.py:349
  12.7 0.8 copy-start.3
  12.7 1.1 %copy-start.4 = (bf16[128,128]{1,0:T(8,128)(2,1)S(1)}, bf16[128,128]{1,0:T(8,128)(2,1)}, u32[]{:S(2)}) copy-start(bf16[128,128]{1,0:T(8,128)(2,1)} %values_ref.1) | copy-start | bytes 98308
  12.7 1.2 %copy-start.2 = (bf16[128,1024]{1,0:T(8,128)(2,1)S(1)}, bf16[128,1024]{1,0:T(8,128)(2,1)}, u32[]{:S(2)}) copy-start(bf16[128,1024]{1,0:T(8,128)(2,1)} %queries_ref.1) | copy-start | bytes 786436
  12.8 1.0 %copy-start.1 = (bf16[128,128]{1,0:T(8,128)(2,1)S(1)}, bf16[128,128]{1,0:T(8,128)(2,1)}, u32[]{:S(2)}) copy-start(bf16[128,128]{1,0:T(8,128)(2,1)} %keys_ref.5) | copy-start | bytes 98308

commit v9 on v7

--- a/solution.py
+++ b/solution.py
@@ -17,7 +17,7 @@
 PANEL = 40
 STRIP = 8
 AHEAD = 5
-TOGETHER = 2
+TOGETHER = 4
 PIECE = 16
 UNIT = 16
 SLOTS = 7

time: 89.5 us -> 89.2 us (level)
  no operation moved by 1% of the time
where the time goes in v9:
time: 89.2 us; the launch traced here: 88.8 us
  blocking collectives  64.5 us (72%)
  starting transfers between devices  10.1 us (11%)
  Pallas kernels  8.56 us (10%)
  waiting for transfers between devices  3.07 us (3%)
  local copies, waits for them, and re-layouts  1.38 us (2%)
    all_to_all x1, blocking collectives, on_device(): lax.all_to_all(second, ('far', 'near'), 0, 0, axis_index_groups=groups)  29.7 us
    all_to_all x1, blocking collectives, on_device(): third = lax.all_to_all(third, near_axes, 0, 0)  23.5 us
    all_to_all x1, blocking collectives, on_device(): first = lax.all_to_all(first, near_axes, 0, 0)  11.3 us
    all_to_all x1, starting transfers between devices, on_device(): pivots = lax.all_to_all(pivots, 'head', 0, 0)  10.1 us
    pallas_call x8, Pallas kernels, call(): pl.pallas_call(kernel, out_shape=out_shape, in_specs=[smem] * scalars + [...  8.56 us
    all_to_all x1, waiting for transfers between devices, on_device(): pivots = lax.all_to_all(pivots, 'head', 0, 0)  3.07 us
  transfers between devices with their start and end apart: 1, of which 1 were waited for; matrix products, arithmetic and copies ran while one was open for 0% of the time, Pallas kernels for 1%

profile of v9, /device:TPU:1, one launch (start us, length us, event | category | flops | bytes accessed | tf_op | source)
XLA Modules:
  0.0 88.8 jit_solution(2849098239166060171)
XLA Ops:
  0.6 0.0 copy-start
  0.6 0.7 copy-done
  1.4 0.8 pivots.1
  2.2 10.1 %all-to-all-start = ((bf16[8,32,128]{2,1,0:T(8,128)(2,1)}), bf16[8,32,128]{2,1,0:T(8,128)(2,1)S(1)}, u32[]{:S(2)}, u32[]{:S(2)}) async-start(bf16[8,32,128]{2,1,0:T(8,128)(2,1)} %pivots.1), calls=%async_computation | async-start | bytes 131072 | tf_op jit(solution)/shard_map/all_to_all | solution.py:349
  12.3 0.3 fusion
  12.7 0.0 copy-start.3
  12.7 0.0 copy-start.4
  12.7 0.0 copy-start.2
  12.7 0.1 pad_maximum_fusion
  12.8 0.0 copy-start.1
  12.8 0.6 copy-done.3
  13.4 0.3 index.1.place_ref
  13.7 0.0 copy-done.4
  13.8 0.0 copy-done.1
  13.8 0.1 prepare.1.kv_ref
  13.9 0.0 copy-done.2
  13.9 0.2 queries.1
  14.1 3.1 %all-to-all-done.piv_ref = bf16[8,32,128]{2,1,0:T(8,128)(2,1)S(1)} async-done(((bf16[8,32,128]{2,1,0:T(8,128)(2,1)}), bf16[8,32,128]{2,1,0:T(8,128)(2,1)S(1)}, u32[]{:S(2)}, u32[]{:S(2)}) %all-to-all-start) | async-done | bytes 65568 | tf_op jit(solution)/shard_map/all_to_all | solution.py:349
  17.2 0.5 sums.1
  17.7 11.3 %all_to_all.20.in_ref = bf16[16,48,128]{2,1,0:T(8,128)(2,1)S(1)} all-to-all(bf16[16,48,128]{2,1,0:T(8,128)(2,1)S(1)} %get-tuple-element.26), channel_id=1, replica_groups=mesh['x'=4,'far'=4,'near'=4,'head'=8] {'x','near'}, dimensions={0} | all-to-all | bytes 393216 | tf_op jit(solution)/shard_map/all_to_all | solution.py:373
  29.0 0.1 middle.1
  29.1 29.7 %all_to_all.21 = bf16[4,288,128]{2,1,0:T(8,128)(2,1)S(1)} all-to-all(bf16[4,288,128]{2,1,0:T(8,128)(2,1)S(1)} %middle.1), channel_id=1, replica_groups={{0,32,80,112},{8,40,88,120},{16,48,64,96},{24,56,72,104},{1,33,81,113},..., dimensions={0} | all-to-all | bytes 589824 | tf_op jit(solution)/shard_map/all_to_all | solution.py:378
  58.7 0.8 pick.1
  59.5 23.5 %all_to_all.22.in_ref = bf16[16,144,128]{2,1,0:T(8,128)(2,1)S(1)} all-to-all(bf16[16,144,128]{2,1,0:T(8,128)(2,1)S(1)} %pick.1), channel_id=1, replica_groups=mesh['x'=4,'far'=4,'near'=4,'head'=8] {'x','near'}, dimensions={0} | all-to-all | bytes 1179648 | tf_op jit(solution)/shard_map/all_to_all | solution.py:383
  83.1 5.8 %finish.1 = (bf16[128,1024]{1,0:T(8,128)(2,1)}, f32[160,128]{1,0:T(8,128)}, f32[160,128]{1,0:T(8,128)}) custom-call(s32[1]{0:T(128)} %bitcast.far_ref, s32[1]{0:T(128)} %bitcast.2.head_ref, bf16[1024,128]{1,0:T(8,128)(2,1)S(1)} %get-tuple-element.21.queries_ref, f32[128,1024]{1,0:T(8,128)S(1)} %get-tuple-element.22.bias_ref, ...), custom_call_target="tpu_custom_call" | custom-call | tf_op jit(solution)/shard_map/finish/pallas_call | solution.py:339
  (2 shorter events, 0.0 us)
Async XLA Ops:
  0.6 0.8 copy-start
  2.2 15.0 %all-to-all-start = ((bf16[8,32,128]{2,1,0:T(8,128)(2,1)}), bf16[8,32,128]{2,1,0:T(8,128)(2,1)S(1)}, u32[]{:S(2)}, u32[]{:S(2)}) async-start(bf16[8,32,128]{2,1,0:T(8,128)(2,1)} %pivots.1), calls=%async_computation | async-start | bytes 131072 | tf_op jit(solution)/shard_map/all_to_all | solution.py:349
  12.7 0.8 copy-start.3
  12.7 1.1 %copy-start.4 = (bf16[128,128]{1,0:T(8,128)(2,1)S(1)}, bf16[128,128]{1,0:T(8,128)(2,1)}, u32[]{:S(2)}) copy-start(bf16[128,128]{1,0:T(8,128)(2,1)} %values_ref.1) | copy-start | bytes 98308
  12.7 1.2 %copy-start.2 = (bf16[128,1024]{1,0:T(8,128)(2,1)S(1)}, bf16[128,1024]{1,0:T(8,128)(2,1)}, u32[]{:S(2)}) copy-start(bf16[128,1024]{1,0:T(8,128)(2,1)} %queries_ref.1) | copy-start | bytes 786436
  12.8 1.0 %copy-start.1 = (bf16[128,128]{1,0:T(8,128)(2,1)S(1)}, bf16[128,128]{1,0:T(8,128)(2,1)}, u32[]{:S(2)}) copy-start(bf16[128,128]{1,0:T(8,128)(2,1)} %keys_ref.5) | copy-start | bytes 98308
